TPU v7x, 512 devices: a whole 4x8x8 slice. The times are simulated.
512 devices in a mesh: lon: 32 (over y, x_lo, core), lat: 16 (over z, x_hi).
Axes of the slice: x: 4 (x_hi: 2, x_lo: 2; x = x_hi * 2 + x_lo), y: 8, z: 8, core: 2. Of those that a mesh axis runs over, the one named last changes fastest.
Arguments:
- height_old: float32 [4096, 2048], P('lon', 'lat'), may hold values from -6 to 6
- height_now: float32 [4096, 2048], P('lon', 'lat'), may hold values from -6 to 6
- zonal_old: float32 [4096, 2048], P('lon', 'lat'), may hold values from -6 to 6
- zonal_now: float32 [4096, 2048], P('lon', 'lat'), may hold values from -6 to 6
- meridional_old: float32 [4096, 2048], P('lon', 'lat'), may hold values from -6 to 6
- meridional_now: float32 [4096, 2048], P('lon', 'lat'), may hold values from -6 to 6
- ocean_depth: float32 [4096, 2048], P('lon', 'lat'), may hold values from 0.2 to 1
- land_sea: int32 [4096, 2048], P('lon', 'lat'), may hold values 0 or 1
- metric_factor: float32 [2048], P('lat'), may hold values from 0.5 to 2
- coriolis: float32 [2048], P('lat'), may hold values from -0.5 to 0.5
- implicit_weight: float32 [2048], replicated, may hold values from 150 to 40000
- source_longitude: int32 [512], replicated, may hold values from 0 to 4095
- source_latitude: int32 [512], replicated, may hold values from 0 to 2047
- source_amplitude: float32 [512], replicated, may hold values from -24 to 24
Outputs:
- height_final: float32 [4096, 2048], P('lon', 'lat')
- zonal_final: float32 [4096, 2048], P('lon', 'lat')
- meridional_final: float32 [4096, 2048], P('lon', 'lat')
Inputs may be any that keep to these rules, and one draw needn't show every extreme that they name: `source_longitude`: cells may repeat.
All inputs are finite; a program needn't handle non-finite values. No bound on the sum of `land_sea` on one device may be relied on, other than what follows from the above.
Results may differ from a plain program's by a relative error of at most 0.0003.
Values sent between devices are 32-bit elements; how exact they have to be, the bound alone decides.
No kernel may reach another device: no remote copies, remote signals or barrier semaphores. Data moves between devices by JAX's collectives and lax.ppermute only.
A program may use at most 64 MiB of HBM per device.

v0:
```python
import jax
import jax.numpy as jnp
from jax import lax
from jax.sharding import PartitionSpec as P

COURANT = 0.25


def extended(block, sides, width, periodic):
    for axis, dim in sides:
        count = lax.axis_size(axis)
        forward = [(i, i + 1) for i in range(count - 1)]
        if periodic:
            forward.append((count - 1, 0))
        backward = [(target, source) for source, target in forward]
        low = lax.ppermute(
            lax.slice_in_dim(block, block.shape[dim] - width, None, axis=dim), axis, forward
        )
        high = lax.ppermute(lax.slice_in_dim(block, 0, width, axis=dim), axis, backward)
        block = jnp.concatenate([low, block, high], axis=dim)
    return block


def sent_to_all(shard, axis):
    size = lax.axis_size(axis)
    return lax.all_to_all(
        jnp.broadcast_to(shard[None], (size, *shard.shape)), axis, 0, 0, tiled=True
    )


def joined_along(pieces, dim):
    shape = list(pieces.shape[1:])
    shape[dim] *= pieces.shape[0]
    return jnp.moveaxis(pieces, 0, dim).reshape(shape)


def gathered_copies(shard, axis, dim):
    pieces = sent_to_all(shard, axis)
    return joined_along(pieces, dim)


def solve_lines(lower, middle, upper, rhs):
    target = rhs.shape
    solved = lax.linalg.tridiagonal_solve(
        jnp.broadcast_to(lower, target),
        jnp.broadcast_to(middle, target),
        jnp.broadcast_to(upper, target),
        rhs[..., None],
    )
    return solved[..., 0]


def following(values):
    return jnp.concatenate([values[1:], jnp.zeros_like(values[:1])], axis=0)


def pick_row(values, index_value):
    return lax.dynamic_index_in_dim(values, index_value, 0, keepdims=False)


def per_device(
    height_old,
    height_now,
    zonal_old,
    zonal_now,
    meridional_old,
    meridional_now,
    ocean_depth,
    land_sea,
    metric_factor,
    coriolis,
    implicit_weight,
    source_longitude,
    source_latitude,
    source_amplitude,
):
    columns = height_old.shape[0]
    rows_local = height_old.shape[1]
    wetness = land_sea.astype(height_old.dtype)
    metric = metric_factor[None, :]
    turning = coriolis[None, :]
    first_east = lax.axis_index("lon") * columns
    first_north = lax.axis_index("lat") * rows_local
    east_local = source_longitude - first_east
    north_local = source_latitude - first_north
    inside = (
        (east_local >= 0) & (east_local < columns) & (north_local >= 0) & (north_local < rows_local)
    )
    east_index = jnp.clip(east_local, 0, columns - 1)
    north_index = jnp.clip(north_local, 0, rows_local - 1)
    amounts = jnp.where(inside, source_amplitude, jnp.zeros_like(source_amplitude))
    block_count = lax.axis_size("lat")
    block_index = lax.axis_index("lat")
    blocks_weight = implicit_weight.reshape(block_count, rows_local)
    inner_weight = blocks_weight[:, :-1]
    edge_weight = blocks_weight[:, -1]
    inner_count = rows_local - 1
    position = jnp.arange(inner_count)
    inner_lower = jnp.where(position[None, :] > 0, -inner_weight, jnp.zeros_like(inner_weight))
    inner_upper = jnp.where(
        position[None, :] < inner_count - 1, -inner_weight, jnp.zeros_like(inner_weight)
    )
    inner_middle = 1.0 + 2.0 * inner_weight
    unit_columns = jnp.stack([position == 0, position == inner_count - 1], axis=-1).astype(
        implicit_weight.dtype
    )
    unit_columns = jnp.broadcast_to(unit_columns, (block_count, inner_count, 2))
    responses = lax.linalg.tridiagonal_solve(inner_lower, inner_middle, inner_upper, unit_columns)
    from_below = responses[..., 0]
    from_above = responses[..., 1]
    block_ids = jnp.arange(block_count)
    link_below = jnp.where(block_ids > 0, -inner_weight[:, 0], jnp.zeros_like(edge_weight))
    link_above = -inner_weight[:, -1]
    edge_down = -edge_weight
    edge_up = jnp.where(block_ids < block_count - 1, -edge_weight, jnp.zeros_like(edge_weight))
    reduced_lower = -edge_down * link_below * from_below[:, -1]
    reduced_middle = (
        1.0
        + 2.0 * edge_weight
        - edge_down * link_above * from_above[:, -1]
        - edge_up * following(link_below) * following(from_below[:, 0])
    )
    reduced_upper = -edge_up * following(link_above) * following(from_above[:, 0])
    own_lower = pick_row(inner_lower, block_index)
    own_middle = pick_row(inner_middle, block_index)
    own_upper = pick_row(inner_upper, block_index)
    own_below = pick_row(from_below, block_index)
    own_above = pick_row(from_above, block_index)
    own_link_below = pick_row(link_below, block_index)
    own_link_above = pick_row(link_above, block_index)
    own_edge_down = pick_row(edge_down, block_index)
    flux_east = ocean_depth * wetness * zonal_now
    flux_north = ocean_depth * wetness * meridional_now
    padded_east = extended(jnp.stack([height_now, flux_east]), (("lon", 1),), 1, True)
    padded_north = extended(jnp.stack([height_now, flux_north]), (("lat", 2),), 1, False)
    across_east = padded_east[:, 2:, :] - padded_east[:, :-2, :]
    across_north = padded_north[:, :, 2:] - padded_north[:, :, :-2]
    interim = height_old - COURANT * (metric * across_east[1] + across_north[1])
    interim = interim.at[east_index, north_index].add(amounts)
    zonal_next = wetness * (
        zonal_old - COURANT * metric * across_east[0] + turning * meridional_now
    )
    meridional_next = wetness * (meridional_old - COURANT * across_north[0] - turning * zonal_now)
    partial_value = solve_lines(own_lower, own_middle, own_upper, interim[:, :-1])
    edge_rhs = interim[:, -1] - own_edge_down * partial_value[:, -1]
    packed = jnp.stack([edge_rhs, partial_value[:, 0]])[:, None, :]
    boundary = gathered_copies(packed, "lat", 1)
    reduced_rhs = boundary[0] - edge_up[:, None] * following(boundary[1])
    separators = lax.linalg.tridiagonal_solve(
        reduced_lower, reduced_middle, reduced_upper, reduced_rhs
    )
    stacked = jnp.concatenate([jnp.zeros_like(separators[:1]), separators], axis=0)
    below_edge = pick_row(stacked, block_index)
    own_edge = pick_row(stacked, block_index + 1)
    inner_solved = (
        partial_value
        - own_link_below * below_edge[:, None] * own_below[None, :]
        - own_link_above * own_edge[:, None] * own_above[None, :]
    )
    solved = jnp.concatenate([inner_solved, own_edge[:, None]], axis=1)
    height_next = wetness * solved
    return (height_next, zonal_next, meridional_next)


def solution(mesh):
    placed = (
        P("lon", "lat"),
        P("lon", "lat"),
        P("lon", "lat"),
        P("lon", "lat"),
        P("lon", "lat"),
        P("lon", "lat"),
        P("lon", "lat"),
        P("lon", "lat"),
        P("lat"),
        P("lat"),
        P(),
        P(),
        P(),
        P(),
    )
    return jax.shard_map(
        per_device,
        mesh=mesh,
        in_specs=placed,
        out_specs=(P("lon", "lat"), P("lon", "lat"), P("lon", "lat")),
        check_vma=False,
    )
```

profile of v0, /device:TPU:31, one launch (start us, length us, event | category | flops | bytes accessed | tf_op | source)
XLA Modules:
  0.0 286.2 jit_solution(4796544358127819784)
XLA Ops:
  0.6 0.9 multiply_bitcast_fusion
  1.7 4.8 %collective-permute-start.3 = (f32[2,128,1]{2,1,0:T(8,128)S(1)}, f32[2,128,1]{2,1,0:T(8,128)S(1)}, u32[]{:S(2)}, u32[]{:S(2)}) collective-permute-start(f32[2,128,1]{2,1,0:T(8,128)S(1)} %get-tuple-element.1260), channel_id=1, source_target_pairs={{0,1},{1,2},{2,3},{3,4},{4,5},{5,6},{6,7},{7,8},{8,9},{9,10},{10,1... | collective-permute-start | bytes 3080 | tf_op jit(solution)/shard_map/ppermute | solution.py:16
  6.5 1.9 collective-permute-start.2
  15.3 4.7 %while.66 = (s32[]{:T(128)}, f32[16]{0:T(128)S(1)}, f32[16,2]{0,1:T(2,128)S(1)}, f32[3,32,16]{2,1,0:T(8,128)S(1)}, f32[3,32,16,2]{2,3,1,0:T(2,128)S(1)}, /*index...) while((s32[]{:T(128)}, f32[16]{0:T(128)S(1)}, ...), condition=%wide.region_6.7_spmd, body=%wide.region_5.6_spmd.sunk | while | flops 4737 | bytes 277481 | solution.py:108
  31.1 2.9 %while.67 = (s32[]{:T(128)}, f32[16,2]{0,1:T(2,128)S(1)}, f32[3,32,16,2]{2,3,1,0:T(2,128)S(1)}, f32[3,32,16,2]{2,3,1,0:T(2,128)S(1)}, f32[3,32,16]{2,1,0:T(8,128...) while((s32[]{:T(128)}, f32[16,2]{0,1:T(2,128)S(1)}, ...), condition=%wide.region_8.9_spmd, body=%wide.region_7.8_spmd.sunk | while | flops 3041 | bytes 179861 | solution.py:108
  37.3 0.9 concatenate.104
  44.9 5.8 %collective-permute-start.1 = (f32[2,1,128]{2,1,0:T(1,128)S(1)}, f32[2,1,128]{2,1,0:T(1,128)S(1)}, u32[]{:S(2)}, u32[]{:S(2)}) collective-permute-start(f32[2,1,128]{2,1,0:T(1,128)S(1)} %get-tuple-element.1258), channel_id=1, source_target_pairs={{0,16},{16,32},{32,48},{48,64},{64,80},{80,96},{96,112},{112,128},... | collective-permute-start | bytes 3080 | tf_op jit(solution)/shard_map/ppermute | solution.py:16
  50.7 2.1 collective-permute-start
  55.1 2.6 collective-permute-done
  58.4 25.2 %scatter_fusion = f32[128,128]{1,0:T(8,128)S(1)} fusion(f32[128,128]{1,0:T(8,128)S(1)} %get-tuple-element.1256, s32[512]{0:T(512)S(1)} %bitcast.4474, f32[512]{0:T(512)S(1)} %and_select_fusion), kind=kCustom, calls=%fused_computation | custom fusion | flops 512 | bytes 10240 | tf_op jit(solution)/shard_map/scatter-add | solution.py:139
  83.6 0.8 fusion.721
  88.6 78.2 %while.64 = (s32[]{:T(128)}, f32[128]{0:T(128)S(1)}, f32[128,1]{0,1:T(1,128)S(1)}, f32[3,32,128]{2,1,0:T(8,128)S(1)}, f32[3,32,128,1]{2,1,3,0:T(8,128)S(1)}, /*i...) while((s32[]{:T(128)}, f32[128]{0:T(128)S(1)}, ...), condition=%wide.region_2.3_spmd, body=%wide.region_1.2_spmd.sunk | while | flops 32801 | bytes 280677 | solution.py:44
  92.5 0.8 constant_dynamic-update-slice_fusion.272
  95.6 0.8 constant_dynamic-update-slice_fusion.276
  96.4 0.8 constant_dynamic-update-slice_fusion.277
  97.3 0.8 constant_dynamic-update-slice_fusion.278
  98.1 0.8 constant_dynamic-update-slice_fusion.279
  98.9 0.8 constant_dynamic-update-slice_fusion.280
  99.7 0.8 constant_dynamic-update-slice_fusion.281
  100.6 0.8 constant_dynamic-update-slice_fusion.282
  108.4 0.8 constant_dynamic-update-slice_fusion.292
  109.2 0.8 constant_dynamic-update-slice_fusion.293
  110.0 0.8 constant_dynamic-update-slice_fusion.294
  110.9 0.8 constant_dynamic-update-slice_fusion.295
  111.7 0.8 constant_dynamic-update-slice_fusion.296
  112.5 0.8 constant_dynamic-update-slice_fusion.297
  113.3 0.8 fusion.1182
  129.8 0.8 constant_dynamic-update-slice_fusion.286
  130.5 0.8 constant_dynamic-update-slice_fusion.287
  131.3 0.8 constant_dynamic-update-slice_fusion.288
  132.1 0.8 constant_dynamic-update-slice_fusion.289
  132.9 0.8 constant_dynamic-update-slice_fusion.290
  148.6 0.8 constant_dynamic-update-slice_fusion.277
  149.4 0.8 constant_dynamic-update-slice_fusion.278
  150.2 0.8 constant_dynamic-update-slice_fusion.279
  151.0 0.8 constant_dynamic-update-slice_fusion.280
  151.8 0.8 constant_dynamic-update-slice_fusion.281
  152.6 0.8 constant_dynamic-update-slice_fusion.282
  155.7 0.8 constant_dynamic-update-slice_fusion.286
  156.5 0.8 constant_dynamic-update-slice_fusion.287
  157.3 0.8 constant_dynamic-update-slice_fusion.288
  158.1 0.8 constant_dynamic-update-slice_fusion.289
  158.9 0.8 constant_dynamic-update-slice_fusion.290
  166.8 55.6 %fusion.841 = (f32[128,1]{0,1:T(1,128)S(1)}, f32[128,1]{0,1:T(1,128)S(1)}, f32[128,1]{0,1:T(1,128)S(1)}, f32[128,1]{0,1:T(1,128)S(1)}, f32[128,1]{0,1:T(1,128)S(...) fusion(f32[128]{0:T(128)S(1)} %get-tuple-element.445, ...), kind=kLoop, calls=%fused_computation.1870 | loop fusion | flops 22912 | bytes 46948 | tf_op jit(solution)/shard_map/vmap()/eval_jaxpr/div | solution.py:44
  222.6 2.1 while.65
  230.5 13.0 %all-to-all-start = ((f32[16,2,1,128]{3,2,1,0:T(1,128)}), f32[16,2,1,128]{3,2,1,0:T(1,128)S(1)}, u32[]{:S(2)}, u32[]{:S(2)}) async-start(f32[16,2,1,128]{3,2,1,0:T(1,128)} %broadcast_in_dim.1997), calls=%async_computation | async-start | bytes 32768 | tf_op jit(solution)/shard_map/all_to_all | solution.py:26
  273.8 9.3 %fusion.738 = (f32[1,128]{1,0:T(1,128)S(1)}, f32[1,128]{1,0:T(1,128)S(1)}, f32[1,128]{1,0:T(1,128)S(1)}, f32[1,128]{1,0:T(1,128)S(1)}, f32[1,128]{1,0:T(1,128)S(...) fusion(f32[16,128]{1,0:T(8,128)S(1)} %multiply_subtract_fusion., ...), kind=kLoop, calls=%fused_computation.1663 | loop fusion | flops 5504 | bytes 15476 | tf_op jit(solution)/shard_map/eval_jaxpr/div | solution.py:149
  283.9 1.3 fusion.733
  (694 shorter events, 103.8 us)
Async XLA Ops:
  0.6 1.0 copy-start
  1.7 41.6 %collective-permute-start.3 = (f32[2,128,1]{2,1,0:T(8,128)S(1)}, f32[2,128,1]{2,1,0:T(8,128)S(1)}, u32[]{:S(2)}, u32[]{:S(2)}) collective-permute-start(f32[2,128,1]{2,1,0:T(8,128)S(1)} %get-tuple-element.1260), channel_id=1, source_target_pairs={{0,1},{1,2},{2,3},{3,4},{4,5},{5,6},{6,7},{7,8},{8,9},{9,10},{10,1... | collective-permute-start | bytes 3080 | tf_op jit(solution)/shard_map/ppermute | solution.py:16
  6.5 36.8 %collective-permute-start.2 = (f32[2,128,1]{2,1,0:T(8,128)S(1)}, f32[2,128,1]{2,1,0:T(8,128)S(1)}, u32[]{:S(2)}, u32[]{:S(2)}) collective-permute-start(f32[2,128,1]{2,1,0:T(8,128)S(1)} %get-tuple-element.1259), channel_id=1, source_target_pairs={{1,0},{2,1},{3,2},{4,3},{5,4},{6,5},{7,6},{8,7},{9,8},{10,9},{11,1... | collective-permute-start | bytes 3080 | tf_op jit(solution)/shard_map/ppermute | solution.py:19
  8.5 0.7 copy-start.4
  38.8 0.7 copy-start.13
  39.4 0.7 copy-start.10
  39.4 0.7 copy-start.9
  40.1 0.7 copy-start.11
  43.3 0.8 copy-start.1
  43.3 0.9 copy-start.2
  43.3 0.9 copy-start.5
  43.3 0.9 copy-start.6
  43.3 0.9 copy-start.12
  44.9 10.2 %collective-permute-start.1 = (f32[2,1,128]{2,1,0:T(1,128)S(1)}, f32[2,1,128]{2,1,0:T(1,128)S(1)}, u32[]{:S(2)}, u32[]{:S(2)}) collective-permute-start(f32[2,1,128]{2,1,0:T(1,128)S(1)} %get-tuple-element.1258), channel_id=1, source_target_pairs={{0,16},{16,32},{32,48},{48,64},{64,80},{80,96},{96,112},{112,128},... | collective-permute-start | bytes 3080 | tf_op jit(solution)/shard_map/ppermute | solution.py:16
  50.7 7.0 %collective-permute-start = (f32[2,1,128]{2,1,0:T(1,128)S(1)}, f32[2,1,128]{2,1,0:T(1,128)S(1)}, u32[]{:S(2)}, u32[]{:S(2)}) collective-permute-start(f32[2,1,128]{2,1,0:T(1,128)S(1)} %get-tuple-element.1257), channel_id=1, source_target_pairs={{16,0},{32,16},{48,32},{64,48},{80,64},{96,80},{112,96},{128,112},... | collective-permute-start | bytes 3080 | tf_op jit(solution)/shard_map/ppermute | solution.py:19
  55.0 2.7 copy-start.3
  55.0 2.7 copy-start.7
  55.1 2.7 copy-start.8
  230.5 43.2 %all-to-all-start = ((f32[16,2,1,128]{3,2,1,0:T(1,128)}), f32[16,2,1,128]{3,2,1,0:T(1,128)S(1)}, u32[]{:S(2)}, u32[]{:S(2)}) async-start(f32[16,2,1,128]{3,2,1,0:T(1,128)} %broadcast_in_dim.1997), calls=%async_computation | async-start | bytes 32768 | tf_op jit(solution)/shard_map/all_to_all | solution.py:26
where the time goes:
time: 291 us; the launch traced here: 286 us
  other arithmetic  182 us (63%)
  local copies, waits for them, and re-layouts  40.6 us (14%)
  between operations  31.6 us (11%)
  starting transfers between devices  27.6 us (9%)
    while x228, other arithmetic  74.8 us
    div x8, other arithmetic, solve_lines(): lax.linalg.tridiagonal_solve(jnp.broadcast_to(lower, target), jnp.broadca...  61 us
    scatter-add x1, other arithmetic, per_device(): interim = interim.at[east_index, north_index].add(amounts)  25.2 us
    all_to_all x1, starting transfers between devices, sent_to_all(): lax.all_to_all(jnp.broadcast_to(shard[None], (size, *shard.shape)), axis,...  13 us
    ppermute x2, starting transfers between devices, extended(): lax.ppermute(lax.slice_in_dim(block, block.shape[dim] - width, None, axis...  10.6 us
    div x1, other arithmetic, per_device(): lax.linalg.tridiagonal_solve(reduced_lower, reduced_middle, reduced_upper...  9.35 us
    broadcast_in_dim x91, local copies, waits for them, and re-layouts, per_device(): lax.linalg.tridiagonal_solve(inner_lower, inner_middle, inner_upper, unit...  8.06 us
    slice x14, local copies, waits for them, and re-layouts, solve_lines(): lax.linalg.tridiagonal_solve(jnp.broadcast_to(lower, target), jnp.broadca...  6.54 us
  transfers between devices with their start and end apart: 5, of which 1 were waited for; matrix products, arithmetic and copies ran while one was open for 12% of the time, Pallas kernels for 0%

commit v1 on v0

v1 whole, which is shorter than its diff:
```python
import jax
import jax.numpy as jnp
from jax import lax
from jax.experimental import pallas as pl
from jax.experimental.pallas import tpu as pltpu
from jax.sharding import PartitionSpec as P

COURANT = 0.25
F32 = jnp.float32
BF16 = jnp.bfloat16
HIGH = lax.Precision.HIGHEST
VMEM = pl.BlockSpec(memory_space=pltpu.VMEM)
HBM = pl.BlockSpec(memory_space=pltpu.HBM)


def iota(shape, dim):
    return lax.broadcasted_iota(jnp.int32, shape, dim)


def dot(a, b, contract, precision=HIGH):
    return lax.dot_general(
        a, b, ((contract[:1], contract[1:]), ((), ())), precision=precision, preferred_element_type=F32
    )


def matmul2(x, y):
    a, b, c, d = x
    e, f, g, h = y
    return a * e + b * g, a * f + b * h, c * e + d * g, c * f + d * h


def product_scan(mats, axis, direction, rescale):
    shape = mats[0].shape
    size = shape[axis]
    place = iota(shape, axis)
    identity = (1.0, 0.0, 0.0, 1.0)
    step = 1
    while step < size:
        if direction == 1:
            keep, shift = place >= step, step
        else:
            keep, shift = place < size - step, size - step
        other = [jnp.where(keep, pltpu.roll(m, shift, axis), i) for m, i in zip(mats, identity)]
        mats = matmul2(mats, other)
        if rescale:
            factor = 1.0 / (mats[0] + mats[1] + mats[2] + mats[3])
            mats = tuple(m * factor for m in mats)
        step *= 2
    return mats


def lane(values, index):
    return jnp.broadcast_to(values[:, index : index + 1], values.shape)


def masked_product(values, low, high):
    row = iota(values.shape, 0)
    kept = jnp.where((row >= low) & (row < high), values, 1.0)
    out = kept[:8]
    for start in range(8, values.shape[0], 8):
        out = out * kept[start : start + 8]
    for step in (4, 2, 1):
        out = out * pltpu.roll(out, step, 0)
    return out


def pick(flag, yes, no):
    return jnp.where(jnp.full((8, 128), flag, jnp.int32) == 1, yes, no)


def rows_of(parts):
    row = iota((8, 128), 0)
    out = jnp.zeros((8, 128), F32)
    for index, part in enumerate(parts):
        out = jnp.where(row == index, part, out)
    return out


def prepare_kernel(*refs):
    sources, (interim_ref, total_ref, vectors_ref, mix_ref, take_ref, wet_ref, zonal_part_ref, meridional_part_ref, border_ref) = refs[:14], refs[14:23]
    held, rows_ref, arrived = refs[23:37], refs[37], refs[38]
    copies = [pltpu.make_async_copy(src, dst, arrived.at[i]) for i, (src, dst) in enumerate(zip(sources, held))]
    for copy in copies:
        copy.start()
    (
        weight_ref,
        lon_ref,
        lat_ref,
        amount_ref,
        height_old_ref,
        height_now_ref,
        zonal_old_ref,
        zonal_ref,
        meridional_old_ref,
        meridional_ref,
        depth_ref,
        land_ref,
        metric_ref,
        coriolis_ref,
    ) = held
    columns, rows = height_now_ref.shape
    blocks = weight_ref.shape[0]
    block = lax.axis_index("lat")
    first_east = lax.axis_index("lon") * columns
    first_north = block * rows

    copies[0].wait()
    c = 1.0 / weight_ref[...]
    one = jnp.ones_like(c)
    mats = (1.0 + c, one, c, one)
    up = product_scan(mats, 1, 1, False)
    down = product_scan(mats, 1, -1, False)
    up_all = tuple(lane(m, rows - 1) for m in up)
    down_all = tuple(lane(m, 0) for m in down)
    factor = 1.0 / (up_all[0] + up_all[1] + up_all[2] + up_all[3])
    ahead = product_scan(tuple(m * factor for m in up_all), 0, 1, True)
    factor = 1.0 / (down_all[0] + down_all[1] + down_all[2] + down_all[3])
    behind = product_scan(tuple(m * factor for m in down_all), 0, -1, True)
    row = iota(c.shape, 0)
    place = iota(c.shape, 1)
    rho = jnp.where(
        row == 0, 1.0, pltpu.roll((ahead[2] + ahead[3]) / (ahead[0] + ahead[1]), 1, 0)
    )
    sigma = jnp.where(
        row == blocks - 1,
        1.0,
        pltpu.roll((behind[2] + behind[3]) / (behind[0] + behind[1]), blocks - 1, 0),
    )
    p_after = up[0] + up[1] * rho
    q_before = down[0] + down[1] * sigma
    p = jnp.where(place == 0, 1.0, pltpu.roll(p_after, 1, 1))
    q = jnp.where(place == rows - 1, 1.0, pltpu.roll(q_before, rows - 1, 1))
    p_end = up_all[0] + up_all[1] * rho
    q_end = down_all[0] + down_all[1] * sigma
    scale = 1.0 / (up_all[2] + up_all[3] * rho + lane(p, rows - 1) * sigma)
    alpha = 1.0 / p_end
    beta = 1.0 / q_end
    c_below = jnp.where(row == 0, 0.0, pltpu.roll(lane(c, rows - 1), 1, 0))
    c_above = jnp.where(row == blocks - 1, 0.0, pltpu.roll(lane(c, 0), blocks - 1, 0))
    low_p = -COURANT * c_below * (1.0 - rho)
    low_q = -COURANT * c_below * q_end
    high_p = COURANT * c_above * p_end
    high_q = COURANT * c_above * (1.0 - sigma)
    stacked = (
        p * c,
        q * c,
        q * scale,
        p * scale,
        low_p * q * scale,
        high_q * p * scale,
        jnp.where(place == 0, low_p, jnp.where(place == rows - 1, high_p, 0.0)),
        jnp.where(place == 0, low_q, jnp.where(place == rows - 1, high_q, 0.0)),
    )
    for index, values in enumerate(stacked):
        rows_ref[index] = values
        vectors_ref[index : index + 1, :] = rows_ref[index, pl.ds(block, 1), :]

    for k in range(blocks.bit_length() - 1):
        size = 1 << k
        bit = (block >> k) & 1
        middle = ((block >> k) + 1 - bit) << k
        to_top = masked_product(alpha, middle - 1, middle + size - 1)
        to_bottom = masked_product(beta, middle - size + 1, middle + 1)
        own_up = masked_product(alpha, middle - 1, block)
        own_down = masked_product(beta, block + 1, middle + 1)
        is_first = (block == middle).astype(F32)
        is_last = (block == middle - 1).astype(F32)
        mine = rows_of((pick(bit, 1.0, to_top), pick(bit, to_bottom, 1.0), pick(bit, 1.0, 0.0), pick(bit, 0.0, 1.0)))
        theirs = rows_of((pick(bit, to_top, 1.0), pick(bit, 1.0, to_bottom), pick(bit, 0.0, 1.0), pick(bit, 1.0, 0.0)))
        take = rows_of((pick(bit, own_up, 0.0), pick(bit, 0.0, own_down), is_first, is_last))
        mix_ref[k, 0:4, :] = mine[0:4]
        mix_ref[k, 4:8, :] = theirs[0:4]
        take_ref[k, 0:4, :] = take[0:4]

    for copy in copies[1:]:
        copy.wait()
    shape = (columns, rows)
    lanes = iota(shape, 1)
    subs = iota(shape, 0)
    added = jnp.zeros(shape, F32)
    for chunk in range(lon_ref.shape[0]):
        amount = amount_ref[chunk : chunk + 1, :]
        here = lon_ref[chunk : chunk + 1, :] - first_east == subs
        there = jnp.where(lat_ref[chunk : chunk + 1, :] - first_north == subs, 1.0, 0.0).astype(BF16)
        for _ in range(3):
            part = amount.astype(BF16).astype(F32)
            amount = amount - part
            added += dot(jnp.where(here, part, 0.0).astype(BF16), there, (1, 1), None)

    wet = land_ref[...].astype(F32)
    depth = depth_ref[...] * wet
    flux_east = depth * zonal_ref[...]
    flux_north = depth * meridional_ref[...]
    across_east = jnp.where(subs == columns - 1, 0.0, pltpu.roll(flux_east, columns - 1, 0)) - jnp.where(
        subs == 0, 0.0, pltpu.roll(flux_east, 1, 0)
    )
    across_north = jnp.where(lanes == rows - 1, 0.0, pltpu.roll(flux_north, rows - 1, 1)) - jnp.where(
        lanes == 0, 0.0, pltpu.roll(flux_north, 1, 1)
    )
    interim = height_old_ref[...] - COURANT * (metric_ref[...] * across_east + across_north) + added
    interim_ref[...] = interim
    vectors = vectors_ref[...]
    border_ref[...] = flux_north[:, 0:1] * vectors[4:5, :] + flux_north[:, rows - 1 : rows] * vectors[5:6, :]

    height = height_now_ref[...]
    turning = coriolis_ref[...]
    across_east = jnp.where(subs == columns - 1, 0.0, pltpu.roll(height, columns - 1, 0)) - jnp.where(
        subs == 0, 0.0, pltpu.roll(height, 1, 0)
    )
    across_north = jnp.where(lanes == rows - 1, 0.0, pltpu.roll(height, rows - 1, 1)) - jnp.where(
        lanes == 0, 0.0, pltpu.roll(height, 1, 1)
    )
    wet_ref[...] = wet
    zonal_part_ref[...] = wet * (
        zonal_old_ref[...] - COURANT * metric_ref[...] * across_east + turning * meridional_ref[...]
    )
    meridional_part_ref[...] = wet * (
        meridional_old_ref[...] - COURANT * across_north - turning * zonal_ref[...]
    )

    eight = iota((8, rows), 0)
    along = iota((8, rows), 1)
    edges = pltpu.roll(vectors, 2, 0)
    on_interim = jnp.where(eight < 2, vectors, 0.0)
    on_flux = jnp.where(eight < 2, edges, 0.0)
    on_height = jnp.where(
        ((eight == 2) & (along == rows - 1)) | ((eight == 3) & (along == 0)), 1.0, 0.0
    )
    total = dot(on_interim, interim, (1, 1)) + dot(on_flux, flux_north, (1, 1))
    total += dot(on_height, height_now_ref[...], (1, 1))
    total_ref[...] = total[0:4]


def local_kernel(
    interim_ref, border_ref, vectors_ref, west_ref, east_ref, metric_ref, wet_ref, part_ref, solved_ref, zonal_ref
):
    shape = interim_ref.shape
    columns, rows = shape
    lanes = iota(shape, 1)
    subs = iota(shape, 0)
    wet = wet_ref[...]
    vectors = vectors_ref[...]
    outer = COURANT * metric_ref[...]
    at_west = jnp.where(subs == 0, outer, 0.0)
    at_east = jnp.where(subs == columns - 1, outer, 0.0)
    zonal_ref[...] = part_ref[...] + wet * (at_west * west_ref[0:1, :] - at_east * east_ref[0:1, :])
    interim = interim_ref[...] + at_west * west_ref[1:2, :] - at_east * east_ref[1:2, :]
    p_from = jnp.broadcast_to(vectors[0:1, :], shape).T
    q_from = jnp.broadcast_to(vectors[1:2, :], shape).T
    green = jnp.where(subs <= lanes, p_from * vectors[2:3, :], q_from * vectors[3:4, :])
    solved_ref[...] = wet * (dot(interim, green, (1, 0)) + border_ref[...])


def finish_kernel(taken_ref, vectors_ref, solved_ref, partial_ref, wet_ref, height_ref, meridional_ref):
    rows = vectors_ref.shape[1]
    four = iota((4, rows), 0)
    along = iota((4, rows), 1)
    taken = taken_ref[...]
    wet = wet_ref[...]
    solutions = jnp.where(four == 0, vectors_ref[2:3, :], jnp.where(four == 1, vectors_ref[3:4, :], 0.0))
    sides = jnp.where(
        (four == 2) & (along == 0),
        COURANT,
        jnp.where((four == 3) & (along == rows - 1), -COURANT, 0.0),
    )
    height_ref[...] = solved_ref[...] + wet * dot(taken, solutions, (0, 0))
    meridional_ref[...] = partial_ref[...] + wet * dot(taken, sides, (0, 0))


def call(kernel, shapes, in_specs, scratch=()):
    outs = [jax.ShapeDtypeStruct(shape, F32) for shape in shapes]
    return pl.pallas_call(
        kernel,
        out_shape=outs,
        in_specs=in_specs,
        out_specs=[VMEM] * len(outs),
        scratch_shapes=list(scratch),
        compiler_params=pltpu.CompilerParams(vmem_limit_bytes=54850 << 10 if kernel is prepare_kernel else 8 << 20),
    )


def per_device(
    height_old,
    height_now,
    zonal_old,
    zonal_now,
    meridional_old,
    meridional_now,
    ocean_depth,
    land_sea,
    metric_factor,
    coriolis,
    implicit_weight,
    source_longitude,
    source_latitude,
    source_amplitude,
):
    columns, rows = height_now.shape
    around = lax.axis_size("lon")
    blocks = lax.axis_size("lat")
    rounds = blocks.bit_length() - 1
    odd = lax.axis_index("lon") % 2 == 1
    metric = metric_factor[None, :]
    turning = coriolis[None, :]

    def outer(index):
        def row(values):
            return lax.slice_in_dim(values, index, index + 1, axis=0)

        flux = row(ocean_depth) * row(land_sea).astype(F32) * row(zonal_now)
        return jnp.concatenate([row(height_now), flux], axis=0)

    first, last = outer(0), outer(columns - 1)
    inner_pairs = [(i, i ^ 1) for i in range(around)]
    outer_pairs = [(i, (i + 1 if i % 2 else i - 1) % around) for i in range(around)]
    from_inner = lax.ppermute(jnp.where(odd, first, last), "lon", inner_pairs)
    from_outer = lax.ppermute(jnp.where(odd, last, first), "lon", outer_pairs)

    read = (
        implicit_weight.reshape(blocks, rows),
        source_longitude.reshape(-1, rows),
        source_latitude.reshape(-1, rows),
        source_amplitude.reshape(-1, rows),
        height_old,
        height_now,
        zonal_old,
        zonal_now,
        meridional_old,
        meridional_now,
        ocean_depth,
        land_sea,
        metric,
        turning,
    )
    block = (columns, rows)
    interim, total, vectors, mix, take, wet, zonal_part, meridional_part, border = call(
        prepare_kernel,
        [block, (4, columns), (8, rows), (rounds, 8, columns), (rounds, 4, columns), block, block, block, block],
        [HBM] * len(read),
        [pltpu.VMEM(x.shape, x.dtype) for x in read]
        + [pltpu.VMEM((8, blocks, rows), F32), pltpu.SemaphoreType.DMA((len(read),))],
    )(*read)

    east = jnp.where(odd, from_outer, from_inner)
    west = jnp.where(odd, from_inner, from_outer)
    weighted = COURANT * metric * vectors[0:2]
    at_west = jnp.sum(weighted * west[1:2], axis=1, keepdims=True)
    at_east = jnp.sum(weighted * east[1:2], axis=1, keepdims=True)
    along = lax.broadcasted_iota(jnp.int32, (2, columns), 1)
    change = jnp.where(along == 0, at_west, 0.0) - jnp.where(along == columns - 1, at_east, 0.0)
    group = jnp.concatenate([total[0:2] + change, total[2:4]], axis=0)

    solved, zonal_next = call(local_kernel, [block] * 2, [VMEM] * 8)(
        interim, border, vectors, west, east, metric, wet, zonal_part
    )

    taken = jnp.zeros_like(group)
    for k in range(rounds):
        size = 1 << k
        mask = size + size // 2 if k == rounds - 1 and k > 1 else size
        theirs = lax.ppermute(group, "lat", [(i, i ^ mask) for i in range(blocks)])
        taken = taken + take[k] * theirs
        group = mix[k, 0:4] * group + mix[k, 4:8] * theirs

    height_next, meridional_next = call(finish_kernel, [block] * 2, [VMEM] * 5)(
        taken, vectors, solved, meridional_part, wet
    )
    return height_next, zonal_next, meridional_next


def solution(mesh):
    grid = P("lon", "lat")
    placed = (grid,) * 8 + (P("lat"), P("lat"), P(), P(), P(), P())
    return jax.shard_map(
        per_device, mesh=mesh, in_specs=placed, out_specs=(grid, grid, grid), check_vma=False
    )
```

time: 291 us -> 44.9 us (0.15)
  the two profiles are of different devices: /device:TPU:31 before, /device:TPU:4 now
where the time goes in v1:
time: 44.9 us; the launch traced here: 44.5 us
  starting transfers between devices  31.4 us (70%)
  waiting for transfers between devices  6.47 us (14%)
  Pallas kernels  4.03 us (9%)
  other arithmetic  1.1 us (2%)
  between operations  0.83 us (2%)
  local copies, waits for them, and re-layouts  0.7 us (2%)
    ppermute x4, starting transfers between devices, per_device(): theirs = lax.ppermute(group, 'lat', [(i, i ^ mask) for i in range(blocks)])  24 us
    ppermute x4, waiting for transfers between devices, per_device(): theirs = lax.ppermute(group, 'lat', [(i, i ^ mask) for i in range(blocks)])  6.46 us
    ppermute x1, starting transfers between devices, per_device(): from_outer = lax.ppermute(jnp.where(odd, last, first), 'lon', outer_pairs)  5.45 us
    pallas_call x1, Pallas kernels, per_device(): call(prepare_kernel, [block, (4, columns), (8, rows), (rounds, 8, columns...  2.25 us
    ppermute x1, starting transfers between devices, per_device(): from_inner = lax.ppermute(jnp.where(odd, first, last), 'lon', inner_pairs)  1.92 us
    pallas_call x1, Pallas kernels, per_device(): call(finish_kernel, [block] * 2, [VMEM] * 5)  0.97 us
  transfers between devices with their start and end apart: 6, of which 4 were waited for; matrix products, arithmetic and copies ran while one was open for 0% of the time, Pallas kernels for 7%

profile of v1, /device:TPU:4, one launch (start us, length us, event | category | flops | bytes accessed | tf_op | source)
XLA Modules:
  0.0 44.5 jit_solution(9571219153280667)
XLA Ops:
  0.6 0.8 %slice_multiply_fusion.2 = (f32[1,128]{1,0:T(1,128)S(1)}, f32[1,128]{1,0:T(1,128)S(1)}, f32[1,128]{1,0:T(1,128)S(1)}, f32[1,128]{1,0:T(1,128)S(1)}) fusion(f32[128,128]{1,0:T(8,128)} %refs_7_.1, s32[128,128]{1,0:T(8,128)} %refs_11_.1, f32[128,128]{1,0:T(8,128)} %refs_10_.1, f32[128,128]{1,0:T(8,128)} %refs_5_.1), kind=kLoop, calls=%fused_computation.31 | loop fusion | flops 768 | bytes 6144 | tf_op jit(solution)/shard_map/mul | solution.py:310
  1.5 0.0 copy-start.4
  1.5 5.5 %collective-permute-start.1 = (f32[2,128]{1,0:T(2,128)S(1)}, f32[2,128]{1,0:T(2,128)S(1)}, u32[]{:S(2)}, u32[]{:S(2)}) collective-permute-start(f32[2,128]{1,0:T(2,128)S(1)} %get-tuple-element.39), channel_id=1, source_target_pairs={{0,496},{16,32},{32,16},{48,64},{64,48},{80,96},{96,80},{112,128},... | collective-permute-start | bytes 3080 | tf_op jit(solution)/shard_map/ppermute | solution.py:317
  6.9 0.0 copy-start
  6.9 1.9 %collective-permute-start = (f32[2,128]{1,0:T(2,128)S(1)}, f32[2,128]{1,0:T(2,128)S(1)}, u32[]{:S(2)}, u32[]{:S(2)}) collective-permute-start(f32[2,128]{1,0:T(2,128)S(1)} %get-tuple-element.40), channel_id=1, source_target_pairs={{0,16},{16,0},{32,48},{48,32},{64,80},{80,64},{96,112},{112,96},{1... | collective-permute-start | bytes 3080 | tf_op jit(solution)/shard_map/ppermute | solution.py:316
  8.9 0.0 copy-done.4
  8.9 0.0 copy-start.3
  8.9 0.0 copy-start.2
  8.9 0.0 copy-start.1
  8.9 0.0 copy-start.5
  9.0 0.0 copy-done
  9.0 0.6 %copy-done.3 = f32[512]{0:T(512)S(1)} copy-done((f32[512]{0:T(512)S(1)}, f32[512]{0:T(512)}, u32[]{:S(2)}) %copy-start.3) | copy-done | bytes 2072
  9.6 0.0 copy-done.2
  9.6 0.0 copy-done.1
  9.6 0.0 copy-done.5
  9.6 2.2 %shard_map.157 = (f32[128,128]{1,0:T(8,128)S(1)}, f32[4,128]{1,0:T(4,128)S(1)}, f32[8,128]{1,0:T(8,128)S(1)}, f32[4,8,128]{2,1,0:T(8,128)S(1)}, f32[4,4,128]{2,1...) custom-call(f32[16,128]{1,0:T(8,128)S(1)} %bitcast.54, ...), custom_call_target="tpu_custom_call" | custom-call | tf_op jit(solution)/shard_map/pallas_call | solution.py:336
  11.9 0.0 collective-permute-done.1
  11.9 0.0 collective-permute-done
  11.9 0.1 multiply_reduce_fusion.1
  12.1 0.1 subtract_add_fusion
  12.2 4.3 %collective-permute-start.2 = (f32[4,128]{1,0:T(4,128)S(1)}, f32[4,128]{1,0:T(4,128)S(1)}, u32[]{:S(2)}, u32[]{:S(2)}) collective-permute-start(f32[4,128]{1,0:T(4,128)S(1)} %pad_maximum_fusion), channel_id=1, source_target_pairs={{0,1},{1,0},{2,3},{3,2},{4,5},{5,4},{6,7},{7,6},{8,9},{9,8},{10,11... | collective-permute-start | bytes 6152 | tf_op jit(solution)/shard_map/ppermute | solution.py:361
  16.5 2.6 %collective-permute-done.2 = f32[4,128]{1,0:T(4,128)S(1)} collective-permute-done((f32[4,128]{1,0:T(4,128)S(1)}, f32[4,128]{1,0:T(4,128)S(1)}, u32[]{:S(2)}, u32[]{:S(2)}) %collective-permute-start.2) | collective-permute-done | bytes 2080 | tf_op jit(solution)/shard_map/ppermute | solution.py:361
  19.2 4.3 %collective-permute-start.3 = (f32[4,128]{1,0:T(4,128)S(1)}, f32[4,128]{1,0:T(4,128)S(1)}, u32[]{:S(2)}, u32[]{:S(2)}) collective-permute-start(f32[4,128]{1,0:T(4,128)S(1)} %fusion.4), channel_id=1, source_target_pairs={{0,2},{1,3},{2,0},{3,1},{4,6},{5,7},{6,4},{7,5},{8,10},{9,11},{10,... | collective-permute-start | bytes 6152 | tf_op jit(solution)/shard_map/ppermute | solution.py:361
  23.5 1.5 %collective-permute-done.3 = f32[4,128]{1,0:T(4,128)S(1)} collective-permute-done((f32[4,128]{1,0:T(4,128)S(1)}, f32[4,128]{1,0:T(4,128)S(1)}, u32[]{:S(2)}, u32[]{:S(2)}) %collective-permute-start.3) | collective-permute-done | bytes 2080 | tf_op jit(solution)/shard_map/ppermute | solution.py:361
  25.0 6.1 %collective-permute-start.4 = (f32[4,128]{1,0:T(4,128)S(1)}, f32[4,128]{1,0:T(4,128)S(1)}, u32[]{:S(2)}, u32[]{:S(2)}) collective-permute-start(f32[4,128]{1,0:T(4,128)S(1)} %fusion.2), channel_id=1, source_target_pairs={{0,4},{1,5},{2,6},{3,7},{4,0},{5,1},{6,2},{7,3},{8,12},{9,13},{10,... | collective-permute-start | bytes 6152 | tf_op jit(solution)/shard_map/ppermute | solution.py:361
  31.1 1.5 %collective-permute-done.4 = f32[4,128]{1,0:T(4,128)S(1)} collective-permute-done((f32[4,128]{1,0:T(4,128)S(1)}, f32[4,128]{1,0:T(4,128)S(1)}, u32[]{:S(2)}, u32[]{:S(2)}) %collective-permute-start.4) | collective-permute-done | bytes 2080 | tf_op jit(solution)/shard_map/ppermute | solution.py:361
  32.7 9.3 %collective-permute-start.5 = (f32[4,128]{1,0:T(4,128)S(1)}, f32[4,128]{1,0:T(4,128)S(1)}, u32[]{:S(2)}, u32[]{:S(2)}) collective-permute-start(f32[4,128]{1,0:T(4,128)S(1)} %fusion), channel_id=1, source_target_pairs={{0,12},{1,13},{2,14},{3,15},{4,8},{5,9},{6,10},{7,11},{8,4},{9,5},... | collective-permute-start | bytes 6152 | tf_op jit(solution)/shard_map/ppermute | solution.py:361
  42.0 0.8 %shard_map.158 = (f32[128,128]{1,0:T(8,128)S(1)}, f32[128,128]{1,0:T(8,128)}) custom-call(f32[128,128]{1,0:T(8,128)S(1)} %get-tuple-element.20.interim_ref, f32[128,128]{1,0:T(8,128)S(1)} %get-tuple-element.21.border_ref, f32[8,128]{1,0:T(8,128)S(1)} %get-tuple-element.18.vectors_ref, f32[2,128]{1,0:T(2,128)S(1)} %get-tuple-element.38.west_ref, ...), custom_call_target="tpu_custom_call" | custom-call | tf_op jit(solution)/shard_map/pallas_call | solution.py:353
  42.8 0.7 %collective-permute-done.5 = f32[4,128]{1,0:T(4,128)S(1)} collective-permute-done((f32[4,128]{1,0:T(4,128)S(1)}, f32[4,128]{1,0:T(4,128)S(1)}, u32[]{:S(2)}, u32[]{:S(2)}) %collective-permute-start.5) | collective-permute-done | bytes 2080 | tf_op jit(solution)/shard_map/ppermute | solution.py:361
  43.5 1.0 %shard_map.159 = (f32[128,128]{1,0:T(8,128)}, f32[128,128]{1,0:T(8,128)}) custom-call(f32[4,128]{1,0:T(4,128)S(1)} %fusion.1.taken_ref, f32[8,128]{1,0:T(8,128)S(1)} %get-tuple-element.18.vectors_ref, f32[128,128]{1,0:T(8,128)S(1)} %get-tuple-element.24.solved_ref, f32[128,128]{1,0:T(8,128)S(1)} %get-tuple-element.25.partial_ref, ...), custom_call_target="tpu_custom_call" | custom-call | tf_op jit(solution)/shard_map/pallas_call | solution.py:365
  (11 shorter events, 0.1 us)
Async XLA Ops:
  1.5 7.4 %copy-start.4 = (f32[128]{0:T(128)S(1)}, f32[128]{0:T(128)}, u32[]{:S(2)}) copy-start(f32[128]{0:T(128)} %param.22) | copy-start | bytes 1540
  1.5 10.4 %collective-permute-start.1 = (f32[2,128]{1,0:T(2,128)S(1)}, f32[2,128]{1,0:T(2,128)S(1)}, u32[]{:S(2)}, u32[]{:S(2)}) collective-permute-start(f32[2,128]{1,0:T(2,128)S(1)} %get-tuple-element.39), channel_id=1, source_target_pairs={{0,496},{16,32},{32,16},{48,64},{64,48},{80,96},{96,80},{112,128},... | collective-permute-start | bytes 3080 | tf_op jit(solution)/shard_map/ppermute | solution.py:317
  6.9 2.0 %copy-start = (f32[2048]{0:T(1024)S(1)}, f32[2048]{0:T(1024)}, u32[]{:S(2)}) copy-start(f32[2048]{0:T(1024)} %param.24) | copy-start | bytes 24580
  6.9 4.9 %collective-permute-start = (f32[2,128]{1,0:T(2,128)S(1)}, f32[2,128]{1,0:T(2,128)S(1)}, u32[]{:S(2)}, u32[]{:S(2)}) collective-permute-start(f32[2,128]{1,0:T(2,128)S(1)} %get-tuple-element.40), channel_id=1, source_target_pairs={{0,16},{16,0},{32,48},{48,32},{64,80},{80,64},{96,112},{112,96},{1... | collective-permute-start | bytes 3080 | tf_op jit(solution)/shard_map/ppermute | solution.py:316
  8.9 0.7 %copy-start.3 = (f32[512]{0:T(512)S(1)}, f32[512]{0:T(512)}, u32[]{:S(2)}) copy-start(f32[512]{0:T(512)} %param.27) | copy-start | bytes 6148
  8.9 0.7 %copy-start.2 = (s32[512]{0:T(512)S(1)}, s32[512]{0:T(512)}, u32[]{:S(2)}) copy-start(s32[512]{0:T(512)} %param.26) | copy-start | bytes 6148
  8.9 0.7 %copy-start.1 = (s32[512]{0:T(512)S(1)}, s32[512]{0:T(512)}, u32[]{:S(2)}) copy-start(s32[512]{0:T(512)} %param.25) | copy-start | bytes 6148
  8.9 0.7 %copy-start.5 = (f32[128]{0:T(128)S(1)}, f32[128]{0:T(128)}, u32[]{:S(2)}) copy-start(f32[128]{0:T(128)} %param.23) | copy-start | bytes 1540
  12.2 7.0 %collective-permute-start.2 = (f32[4,128]{1,0:T(4,128)S(1)}, f32[4,128]{1,0:T(4,128)S(1)}, u32[]{:S(2)}, u32[]{:S(2)}) collective-permute-start(f32[4,128]{1,0:T(4,128)S(1)} %pad_maximum_fusion), channel_id=1, source_target_pairs={{0,1},{1,0},{2,3},{3,2},{4,5},{5,4},{6,7},{7,6},{8,9},{9,8},{10,11... | collective-permute-start | bytes 6152 | tf_op jit(solution)/shard_map/ppermute | solution.py:361
  19.2 5.8 %collective-permute-start.3 = (f32[4,128]{1,0:T(4,128)S(1)}, f32[4,128]{1,0:T(4,128)S(1)}, u32[]{:S(2)}, u32[]{:S(2)}) collective-permute-start(f32[4,128]{1,0:T(4,128)S(1)} %fusion.4), channel_id=1, source_target_pairs={{0,2},{1,3},{2,0},{3,1},{4,6},{5,7},{6,4},{7,5},{8,10},{9,11},{10,... | collective-permute-start | bytes 6152 | tf_op jit(solution)/shard_map/ppermute | solution.py:361
  25.0 7.6 %collective-permute-start.4 = (f32[4,128]{1,0:T(4,128)S(1)}, f32[4,128]{1,0:T(4,128)S(1)}, u32[]{:S(2)}, u32[]{:S(2)}) collective-permute-start(f32[4,128]{1,0:T(4,128)S(1)} %fusion.2), channel_id=1, source_target_pairs={{0,4},{1,5},{2,6},{3,7},{4,0},{5,1},{6,2},{7,3},{8,12},{9,13},{10,... | collective-permute-start | bytes 6152 | tf_op jit(solution)/shard_map/ppermute | solution.py:361
  32.7 10.9 %collective-permute-start.5 = (f32[4,128]{1,0:T(4,128)S(1)}, f32[4,128]{1,0:T(4,128)S(1)}, u32[]{:S(2)}, u32[]{:S(2)}) collective-permute-start(f32[4,128]{1,0:T(4,128)S(1)} %fusion), channel_id=1, source_target_pairs={{0,12},{1,13},{2,14},{3,15},{4,8},{5,9},{6,10},{7,11},{8,4},{9,5},... | collective-permute-start | bytes 6152 | tf_op jit(solution)/shard_map/ppermute | solution.py:361

commit v2 on v1

--- a/solution.py
+++ b/solution.py
@@ -7,6 +7,7 @@
 
 COURANT = 0.25
 F32 = jnp.float32
+PREPARE_LIMIT = 54800 << 10
 BF16 = jnp.bfloat16
 HIGH = lax.Precision.HIGHEST
 VMEM = pl.BlockSpec(memory_space=pltpu.VMEM)
@@ -64,40 +65,45 @@
     return out
 
 
-def pick(flag, yes, no):
-    return jnp.where(jnp.full((8, 128), flag, jnp.int32) == 1, yes, no)
-
-
-def rows_of(parts):
-    row = iota((8, 128), 0)
-    out = jnp.zeros((8, 128), F32)
+def select_rows(row, parts):
+    out = jnp.zeros(row.shape, F32)
     for index, part in enumerate(parts):
         out = jnp.where(row == index, part, out)
     return out
 
 
 def prepare_kernel(*refs):
-    sources, (interim_ref, total_ref, vectors_ref, mix_ref, take_ref, wet_ref, zonal_part_ref, meridional_part_ref, border_ref) = refs[:14], refs[14:23]
-    held, rows_ref, arrived = refs[23:37], refs[37], refs[38]
+    sources, results, held, rows_ref, arrived = refs[:14], refs[14:23], refs[23:37], refs[37], refs[38]
     copies = [pltpu.make_async_copy(src, dst, arrived.at[i]) for i, (src, dst) in enumerate(zip(sources, held))]
     for copy in copies:
         copy.start()
     (
         weight_ref,
+        height_now_ref,
+        zonal_ref,
+        depth_ref,
+        land_ref,
         lon_ref,
         lat_ref,
         amount_ref,
+        meridional_ref,
         height_old_ref,
-        height_now_ref,
-        zonal_old_ref,
-        zonal_ref,
-        meridional_old_ref,
-        meridional_ref,
-        depth_ref,
-        land_ref,
         metric_ref,
         coriolis_ref,
+        zonal_old_ref,
+        meridional_old_ref,
     ) = held
+    (
+        total_ref,
+        vectors_ref,
+        mix_ref,
+        take_ref,
+        wet_ref,
+        zonal_part_ref,
+        meridional_part_ref,
+        green_ref,
+        solved_ref,
+    ) = results
     columns, rows = height_now_ref.shape
     blocks = weight_ref.shape[0]
     block = lax.axis_index("lat")
@@ -155,22 +161,19 @@
         rows_ref[index] = values
         vectors_ref[index : index + 1, :] = rows_ref[index, pl.ds(block, 1), :]
 
+    eight = iota((8, rows), 0)
     for k in range(blocks.bit_length() - 1):
         size = 1 << k
         bit = (block >> k) & 1
         middle = ((block >> k) + 1 - bit) << k
         to_top = masked_product(alpha, middle - 1, middle + size - 1)
         to_bottom = masked_product(beta, middle - size + 1, middle + 1)
-        own_up = masked_product(alpha, middle - 1, block)
-        own_down = masked_product(beta, block + 1, middle + 1)
+        own_up = masked_product(alpha, middle - 1, block) * bit.astype(F32)
+        own_down = masked_product(beta, block + 1, middle + 1) * (1 - bit).astype(F32)
         is_first = (block == middle).astype(F32)
         is_last = (block == middle - 1).astype(F32)
-        mine = rows_of((pick(bit, 1.0, to_top), pick(bit, to_bottom, 1.0), pick(bit, 1.0, 0.0), pick(bit, 0.0, 1.0)))
-        theirs = rows_of((pick(bit, to_top, 1.0), pick(bit, 1.0, to_bottom), pick(bit, 0.0, 1.0), pick(bit, 1.0, 0.0)))
-        take = rows_of((pick(bit, own_up, 0.0), pick(bit, 0.0, own_down), is_first, is_last))
-        mix_ref[k, 0:4, :] = mine[0:4]
-        mix_ref[k, 4:8, :] = theirs[0:4]
-        take_ref[k, 0:4, :] = take[0:4]
+        mix_ref[k] = select_rows(eight, (to_top, 1.0, 0.0, 1.0, 1.0, to_bottom, 1.0, 0.0))
+        take_ref[k] = select_rows(eight, (own_up, 0.0, is_first, 0.0, 0.0, own_down, 0.0, is_last))
 
     for copy in copies[1:]:
         copy.wait()
@@ -198,9 +201,15 @@
         lanes == 0, 0.0, pltpu.roll(flux_north, 1, 1)
     )
     interim = height_old_ref[...] - COURANT * (metric_ref[...] * across_east + across_north) + added
-    interim_ref[...] = interim
+
     vectors = vectors_ref[...]
-    border_ref[...] = flux_north[:, 0:1] * vectors[4:5, :] + flux_north[:, rows - 1 : rows] * vectors[5:6, :]
+    p_from = jnp.broadcast_to(vectors[0:1, :], shape).T
+    q_from = jnp.broadcast_to(vectors[1:2, :], shape).T
+    green = jnp.where(subs <= lanes, p_from * vectors[2:3, :], q_from * vectors[3:4, :])
+    green_ref[...] = green
+    solved = dot(interim, green, (1, 0))
+    solved += flux_north[:, 0:1] * vectors[4:5, :] + flux_north[:, rows - 1 : rows] * vectors[5:6, :]
+    solved_ref[...] = wet * solved
 
     height = height_now_ref[...]
     turning = coriolis_ref[...]
@@ -218,7 +227,6 @@
         meridional_old_ref[...] - COURANT * across_north - turning * zonal_ref[...]
     )
 
-    eight = iota((8, rows), 0)
     along = iota((8, rows), 1)
     edges = pltpu.roll(vectors, 2, 0)
     on_interim = jnp.where(eight < 2, vectors, 0.0)
@@ -231,52 +239,65 @@
     total_ref[...] = total[0:4]
 
 
-def local_kernel(
-    interim_ref, border_ref, vectors_ref, west_ref, east_ref, metric_ref, wet_ref, part_ref, solved_ref, zonal_ref
+def finish_kernel(
+    west_ref,
+    east_ref,
+    metric_ref,
+    vectors_ref,
+    green_ref,
+    wet_ref,
+    zonal_part_ref,
+    meridional_part_ref,
+    solved_ref,
+    take_ref,
+    *refs,
 ):
-    shape = interim_ref.shape
-    columns, rows = shape
-    lanes = iota(shape, 1)
-    subs = iota(shape, 0)
+    gathered, (height_ref, zonal_ref, meridional_ref) = refs[:-3], refs[-3:]
+    columns, rows = wet_ref.shape
     wet = wet_ref[...]
-    vectors = vectors_ref[...]
     outer = COURANT * metric_ref[...]
-    at_west = jnp.where(subs == 0, outer, 0.0)
-    at_east = jnp.where(subs == columns - 1, outer, 0.0)
-    zonal_ref[...] = part_ref[...] + wet * (at_west * west_ref[0:1, :] - at_east * east_ref[0:1, :])
-    interim = interim_ref[...] + at_west * west_ref[1:2, :] - at_east * east_ref[1:2, :]
-    p_from = jnp.broadcast_to(vectors[0:1, :], shape).T
-    q_from = jnp.broadcast_to(vectors[1:2, :], shape).T
-    green = jnp.where(subs <= lanes, p_from * vectors[2:3, :], q_from * vectors[3:4, :])
-    solved_ref[...] = wet * (dot(interim, green, (1, 0)) + border_ref[...])
-
-
-def finish_kernel(taken_ref, vectors_ref, solved_ref, partial_ref, wet_ref, height_ref, meridional_ref):
-    rows = vectors_ref.shape[1]
-    four = iota((4, rows), 0)
-    along = iota((4, rows), 1)
-    taken = taken_ref[...]
-    wet = wet_ref[...]
-    solutions = jnp.where(four == 0, vectors_ref[2:3, :], jnp.where(four == 1, vectors_ref[3:4, :], 0.0))
+    eight = iota((8, rows), 0)
+    along = iota((8, columns), 1)
+
+    zonal_ref[...] = zonal_part_ref[...]
+    last = columns - 1
+    zonal_ref[0:1, :] += wet_ref[0:1, :] * outer * west_ref[0:1, :]
+    zonal_ref[last:columns, :] -= wet_ref[last:columns, :] * outer * east_ref[0:1, :]
+
+    halo = select_rows(eight, (0.0, 0.0, 0.0, 0.0, outer * west_ref[1:2, :], -outer * east_ref[1:2, :]))
+    outer_rows = dot(halo, green_ref[...], (1, 0))
+
+    taken = take_ref[0] * gathered[0][...]
+    for k in range(1, len(gathered)):
+        taken += take_ref[k] * gathered[k][...]
+    taken += pltpu.roll(taken, 4, 0)
+    onto = jnp.where(
+        eight < 4, taken, jnp.where((eight == 4) & (along == 0) | (eight == 5) & (along == last), 1.0, 0.0)
+    )
+    heights = select_rows(
+        eight, (vectors_ref[2:3, :], vectors_ref[3:4, :], 0.0, 0.0, outer_rows, outer_rows)
+    )
     sides = jnp.where(
-        (four == 2) & (along == 0),
-        COURANT,
-        jnp.where((four == 3) & (along == rows - 1), -COURANT, 0.0),
-    )
-    height_ref[...] = solved_ref[...] + wet * dot(taken, solutions, (0, 0))
-    meridional_ref[...] = partial_ref[...] + wet * dot(taken, sides, (0, 0))
-
-
-def call(kernel, shapes, in_specs, scratch=()):
-    outs = [jax.ShapeDtypeStruct(shape, F32) for shape in shapes]
+        (eight == 2) & (along == 0), COURANT, jnp.where((eight == 3) & (along == rows - 1), -COURANT, 0.0)
+    )
+    height_ref[...] = solved_ref[...] + wet * dot(onto, heights, (0, 0))
+    meridional_ref[...] = meridional_part_ref[...] + wet * dot(onto, sides, (0, 0))
+
+
+def call(kernel, shapes, in_specs, scratch=(), limit=8 << 20):
+    outs = [jax.ShapeDtypeStruct(x.shape, x.dtype) for x in shapes]
     return pl.pallas_call(
         kernel,
         out_shape=outs,
         in_specs=in_specs,
         out_specs=[VMEM] * len(outs),
         scratch_shapes=list(scratch),
-        compiler_params=pltpu.CompilerParams(vmem_limit_bytes=54850 << 10 if kernel is prepare_kernel else 8 << 20),
-    )
+        compiler_params=pltpu.CompilerParams(vmem_limit_bytes=limit),
+    )
+
+
+def f32(*shape):
+    return jax.ShapeDtypeStruct(shape, F32)
 
 
 def per_device(
@@ -300,8 +321,8 @@
     blocks = lax.axis_size("lat")
     rounds = blocks.bit_length() - 1
     odd = lax.axis_index("lon") % 2 == 1
+
     metric = metric_factor[None, :]
-    turning = coriolis[None, :]
 
     def outer(index):
         def row(values):
@@ -311,34 +332,36 @@
         return jnp.concatenate([row(height_now), flux], axis=0)
 
     first, last = outer(0), outer(columns - 1)
+
     inner_pairs = [(i, i ^ 1) for i in range(around)]
     outer_pairs = [(i, (i + 1 if i % 2 else i - 1) % around) for i in range(around)]
+    from_outer = lax.ppermute(jnp.where(odd, last, first), "lon", outer_pairs)
     from_inner = lax.ppermute(jnp.where(odd, first, last), "lon", inner_pairs)
-    from_outer = lax.ppermute(jnp.where(odd, last, first), "lon", outer_pairs)
-
+
+    block = f32(columns, rows)
     read = (
         implicit_weight.reshape(blocks, rows),
+        height_now,
+        zonal_now,
+        ocean_depth,
+        land_sea,
         source_longitude.reshape(-1, rows),
         source_latitude.reshape(-1, rows),
         source_amplitude.reshape(-1, rows),
+        meridional_now,
         height_old,
-        height_now,
+        metric,
+        coriolis[None, :],
         zonal_old,
-        zonal_now,
         meridional_old,
-        meridional_now,
-        ocean_depth,
-        land_sea,
-        metric,
-        turning,
-    )
-    block = (columns, rows)
-    interim, total, vectors, mix, take, wet, zonal_part, meridional_part, border = call(
+    )
+    total, vectors, mix, take, wet, zonal_part, meridional_part, green, solved = call(
         prepare_kernel,
-        [block, (4, columns), (8, rows), (rounds, 8, columns), (rounds, 4, columns), block, block, block, block],
+        [f32(4, columns), f32(8, rows), f32(rounds, 8, columns), f32(rounds, 8, columns)] + [block] * 5,
         [HBM] * len(read),
         [pltpu.VMEM(x.shape, x.dtype) for x in read]
         + [pltpu.VMEM((8, blocks, rows), F32), pltpu.SemaphoreType.DMA((len(read),))],
+        PREPARE_LIMIT,
     )(*read)
 
     east = jnp.where(odd, from_outer, from_inner)
@@ -350,20 +373,18 @@
     change = jnp.where(along == 0, at_west, 0.0) - jnp.where(along == columns - 1, at_east, 0.0)
     group = jnp.concatenate([total[0:2] + change, total[2:4]], axis=0)
 
-    solved, zonal_next = call(local_kernel, [block] * 2, [VMEM] * 8)(
-        interim, border, vectors, west, east, metric, wet, zonal_part
-    )
-
-    taken = jnp.zeros_like(group)
+    gathered = []
     for k in range(rounds):
         size = 1 << k
         mask = size + size // 2 if k == rounds - 1 and k > 1 else size
-        theirs = lax.ppermute(group, "lat", [(i, i ^ mask) for i in range(blocks)])
-        taken = taken + take[k] * theirs
-        group = mix[k, 0:4] * group + mix[k, 4:8] * theirs
-
-    height_next, meridional_next = call(finish_kernel, [block] * 2, [VMEM] * 5)(
-        taken, vectors, solved, meridional_part, wet
+        pairs = [[i, i ^ mask] for i in range(blocks) if i < i ^ mask]
+        both = lax.all_gather(group, "lat", axis=0, tiled=True, axis_index_groups=pairs)
+        gathered.append(both)
+        if k < rounds - 1:
+            group = mix[k, 0:4] * both[0:4] + mix[k, 4:8] * both[4:8]
+
+    height_next, zonal_next, meridional_next = call(finish_kernel, [block] * 3, [VMEM] * (10 + rounds))(
+        west, east, metric, vectors, green, wet, zonal_part, meridional_part, solved, take, *gathered
     )
     return height_next, zonal_next, meridional_next
 

time: 44.9 us -> 40.5 us (0.902)
  blocking collectives: 0 us -> 26.7 us
  starting transfers between devices: 31.4 us -> 7.37 us
  waiting for transfers between devices: 6.47 us -> 0.01 us
  Pallas kernels: 4.03 us -> 3.53 us
    all_gather x0 -> x4, blocking collectives: none -> 26.7 us  [per_device(): lax.all_gather(group, 'lat', axis=0, tiled=True, axis_index_groups=pairs)]
    ppermute x4 -> x0, starting transfers between devices: 24 us -> none  [per_device(): theirs = lax.ppermute(group, 'lat', [(i, i ^ mask) for i in range(blocks)])]
    ppermute x4 -> x0, waiting for transfers between devices: 6.46 us -> none  [per_device(): theirs = lax.ppermute(group, 'lat', [(i, i ^ mask) for i in range(blocks)])]
    pallas_call x3 -> x2, Pallas kernels: 4.03 us -> 3.53 us  [the longest x1 2.4 us: per_device(): call(prepare_kernel, [f32(4, columns), f32(8, rows), f32(rounds, 8, colum...]
  transfers between devices with their start and end apart: 6 -> 2, of which waited for: 4 -> 0; matrix products, arithmetic and copies ran while one was open for 0% -> 0% of each run, Pallas kernels for 7% -> 6%
where the time goes in v2:
time: 40.5 us; the launch traced here: 40.2 us
  blocking collectives  26.7 us (66%)
  starting transfers between devices  7.37 us (18%)
  Pallas kernels  3.53 us (9%)
  other arithmetic  1.09 us (3%)
  between operations  0.8 us (2%)
  local copies, waits for them, and re-layouts  0.7 us (2%)
    all_gather x4, blocking collectives, per_device(): lax.all_gather(group, 'lat', axis=0, tiled=True, axis_index_groups=pairs)  26.7 us
    ppermute x1, starting transfers between devices, per_device(): from_outer = lax.ppermute(jnp.where(odd, last, first), 'lon', outer_pairs)  5.45 us
    pallas_call x1, Pallas kernels, per_device(): call(prepare_kernel, [f32(4, columns), f32(8, rows), f32(rounds, 8, colum...  2.4 us
    ppermute x1, starting transfers between devices, per_device(): from_inner = lax.ppermute(jnp.where(odd, first, last), 'lon', inner_pairs)  1.92 us
    pallas_call x1, Pallas kernels, per_device(): call(finish_kernel, [block] * 3, [VMEM] * (10 + rounds))  1.13 us
    mul x1, other arithmetic, outer(): flux = row(ocean_depth) * row(land_sea).astype(F32) * row(zonal_now)  0.81 us
  transfers between devices with their start and end apart: 2, of which 0 were waited for; matrix products, arithmetic and copies ran while one was open for 0% of the time, Pallas kernels for 6%

profile of v2, /device:TPU:4, one launch (start us, length us, event | category | flops | bytes accessed | tf_op | source)
XLA Modules:
  0.0 40.2 jit_solution(16261117464756622305)
XLA Ops:
  0.6 0.8 %slice_multiply_fusion.8 = (f32[1,128]{1,0:T(1,128)S(1)}, f32[1,128]{1,0:T(1,128)S(1)}, f32[1,128]{1,0:T(1,128)S(1)}, f32[1,128]{1,0:T(1,128)S(1)}) fusion(f32[128,128]{1,0:T(8,128)} %refs_2_.1, s32[128,128]{1,0:T(8,128)} %refs_4_.1, f32[128,128]{1,0:T(8,128)} %refs_3_.1, f32[128,128]{1,0:T(8,128)} %refs_1_.1), kind=kLoop, calls=%fused_computation.25 | loop fusion | flops 768 | bytes 6144 | tf_op jit(solution)/shard_map/mul | solution.py:331
  1.5 0.0 copy-start.4
  1.5 5.5 %collective-permute-start.1 = (f32[2,128]{1,0:T(2,128)S(1)}, f32[2,128]{1,0:T(2,128)S(1)}, u32[]{:S(2)}, u32[]{:S(2)}) collective-permute-start(f32[2,128]{1,0:T(2,128)S(1)} %get-tuple-element.31), channel_id=1, source_target_pairs={{0,496},{16,32},{32,16},{48,64},{64,48},{80,96},{96,80},{112,128},... | collective-permute-start | bytes 3080 | tf_op jit(solution)/shard_map/ppermute | solution.py:338
  6.9 0.0 copy-start
  6.9 1.9 %collective-permute-start = (f32[2,128]{1,0:T(2,128)S(1)}, f32[2,128]{1,0:T(2,128)S(1)}, u32[]{:S(2)}, u32[]{:S(2)}) collective-permute-start(f32[2,128]{1,0:T(2,128)S(1)} %get-tuple-element.32), channel_id=1, source_target_pairs={{0,16},{16,0},{32,48},{48,32},{64,80},{80,64},{96,112},{112,96},{1... | collective-permute-start | bytes 3080 | tf_op jit(solution)/shard_map/ppermute | solution.py:339
  8.9 0.0 copy-done.4
  8.9 0.0 copy-start.3
  8.9 0.0 copy-start.2
  8.9 0.0 copy-start.1
  8.9 0.0 copy-start.5
  9.0 0.0 copy-done
  9.0 0.6 %copy-done.3 = f32[512]{0:T(512)S(1)} copy-done((f32[512]{0:T(512)S(1)}, f32[512]{0:T(512)}, u32[]{:S(2)}) %copy-start.3) | copy-done | bytes 2072
  9.6 0.0 copy-done.2
  9.6 0.0 copy-done.1
  9.6 0.0 copy-done.5
  9.6 2.4 %shard_map.157 = (f32[4,128]{1,0:T(4,128)S(1)}, f32[8,128]{1,0:T(8,128)S(1)}, f32[4,8,128]{2,1,0:T(8,128)S(1)}, f32[4,8,128]{2,1,0:T(8,128)S(1)}, f32[128,128]{1...) custom-call(f32[16,128]{1,0:T(8,128)S(1)} %bitcast.20, ...), custom_call_target="tpu_custom_call" | custom-call | tf_op jit(solution)/shard_map/pallas_call | solution.py:358
  12.0 0.0 collective-permute-done.1
  12.0 0.0 collective-permute-done
  12.1 0.1 multiply_reduce_fusion.1
  12.2 0.1 subtract_add_fusion
  12.3 5.8 %all-gather = f32[2,4,128]{2,1,0:T(4,128)S(1)} all-gather(f32[1,4,128]{2,1,0:T(4,128)S(1)} %maximum_bitcast_fusion), channel_id=1, replica_groups={{0,1},{2,3},{4,5},{6,7},{8,9},{10,11},{12,13},{14,15},{16,17},{18,19},{..., dimensions={0}, use_global_device_ids=true | all-gather | bytes 6144 | tf_op jit(solution)/shard_map/all_gather | solution.py:381
  18.2 4.7 %all-gather.1 = f32[2,4,128]{2,1,0:T(4,128)S(1)} all-gather(f32[1,4,128]{2,1,0:T(4,128)S(1)} %fusion.2), channel_id=1, replica_groups={{0,2},{1,3},{4,6},{5,7},{8,10},{9,11},{12,14},{13,15},{16,18},{17,19},{..., dimensions={0}, use_global_device_ids=true | all-gather | bytes 6144 | tf_op jit(solution)/shard_map/all_gather | solution.py:381
  22.9 6.5 %all-gather.2 = f32[2,4,128]{2,1,0:T(4,128)S(1)} all-gather(f32[1,4,128]{2,1,0:T(4,128)S(1)} %fusion.1), channel_id=1, replica_groups={{0,4},{1,5},{2,6},{3,7},{8,12},{9,13},{10,14},{11,15},{16,20},{17,21},{..., dimensions={0}, use_global_device_ids=true | all-gather | bytes 6144 | tf_op jit(solution)/shard_map/all_gather | solution.py:381
  29.3 9.8 %all-gather.3 = f32[2,4,128]{2,1,0:T(4,128)S(1)} all-gather(f32[1,4,128]{2,1,0:T(4,128)S(1)} %fusion), channel_id=1, replica_groups={{0,12},{1,13},{2,14},{3,15},{4,8},{5,9},{6,10},{7,11},{16,28},{17,29},{..., dimensions={0}, use_global_device_ids=true | all-gather | bytes 6144 | tf_op jit(solution)/shard_map/all_gather | solution.py:381
  39.1 1.1 %shard_map.158 = (f32[128,128]{1,0:T(8,128)}, f32[128,128]{1,0:T(8,128)}, f32[128,128]{1,0:T(8,128)}) custom-call(f32[2,128]{1,0:T(2,128)S(1)} %get-tuple-element.30.west_ref, f32[2,128]{1,0:T(2,128)S(1)} %get-tuple-element.29.east_ref, f32[1,128]{1,0:T(1,128)S(1)} %bitcast.25, f32[8,128]{1,0:T(8,128)S(1)} %get-tuple-element.12.vectors_ref, ...), custom_call_target="tpu_custom_call" | custom-call | tf_op jit(solution)/shard_map/pallas_call | solution.py:386
  (10 shorter events, 0.1 us)
Async XLA Ops:
  1.5 7.4 %copy-start.4 = (f32[128]{0:T(128)S(1)}, f32[128]{0:T(128)}, u32[]{:S(2)}) copy-start(f32[128]{0:T(128)} %param.22) | copy-start | bytes 1540
  1.5 10.6 %collective-permute-start.1 = (f32[2,128]{1,0:T(2,128)S(1)}, f32[2,128]{1,0:T(2,128)S(1)}, u32[]{:S(2)}, u32[]{:S(2)}) collective-permute-start(f32[2,128]{1,0:T(2,128)S(1)} %get-tuple-element.31), channel_id=1, source_target_pairs={{0,496},{16,32},{32,16},{48,64},{64,48},{80,96},{96,80},{112,128},... | collective-permute-start | bytes 3080 | tf_op jit(solution)/shard_map/ppermute | solution.py:338
  6.9 2.0 %copy-start = (f32[2048]{0:T(1024)S(1)}, f32[2048]{0:T(1024)}, u32[]{:S(2)}) copy-start(f32[2048]{0:T(1024)} %param.24) | copy-start | bytes 24580
  6.9 5.1 %collective-permute-start = (f32[2,128]{1,0:T(2,128)S(1)}, f32[2,128]{1,0:T(2,128)S(1)}, u32[]{:S(2)}, u32[]{:S(2)}) collective-permute-start(f32[2,128]{1,0:T(2,128)S(1)} %get-tuple-element.32), channel_id=1, source_target_pairs={{0,16},{16,0},{32,48},{48,32},{64,80},{80,64},{96,112},{112,96},{1... | collective-permute-start | bytes 3080 | tf_op jit(solution)/shard_map/ppermute | solution.py:339
  8.9 0.7 %copy-start.3 = (f32[512]{0:T(512)S(1)}, f32[512]{0:T(512)}, u32[]{:S(2)}) copy-start(f32[512]{0:T(512)} %param.27) | copy-start | bytes 6148
  8.9 0.7 %copy-start.2 = (s32[512]{0:T(512)S(1)}, s32[512]{0:T(512)}, u32[]{:S(2)}) copy-start(s32[512]{0:T(512)} %param.26) | copy-start | bytes 6148
  8.9 0.7 %copy-start.1 = (s32[512]{0:T(512)S(1)}, s32[512]{0:T(512)}, u32[]{:S(2)}) copy-start(s32[512]{0:T(512)} %param.25) | copy-start | bytes 6148
  8.9 0.7 %copy-start.5 = (f32[128]{0:T(128)S(1)}, f32[128]{0:T(128)}, u32[]{:S(2)}) copy-start(f32[128]{0:T(128)} %param.23) | copy-start | bytes 1540

commit v3 on v2

v3 whole, which is shorter than its diff:
```python
import jax
import jax.numpy as jnp
from jax import lax
from jax.experimental import pallas as pl
from jax.experimental.pallas import tpu as pltpu
from jax.sharding import PartitionSpec as P

COURANT = 0.25
F32 = jnp.float32
BF16 = jnp.bfloat16
HIGH = lax.Precision.HIGHEST
VMEM = pl.BlockSpec(memory_space=pltpu.VMEM)
HBM = pl.BlockSpec(memory_space=pltpu.HBM)
LIMIT = 8 << 20


def iota(shape, dim):
    return lax.broadcasted_iota(jnp.int32, shape, dim)


def dot(a, b, contract, precision=HIGH):
    return lax.dot_general(
        a, b, ((contract[:1], contract[1:]), ((), ())), precision=precision, preferred_element_type=F32
    )


def matmul2(x, y):
    a, b, c, d = x
    e, f, g, h = y
    return a * e + b * g, a * f + b * h, c * e + d * g, c * f + d * h


def product_scan(mats, axis, direction, rescale):
    shape = mats[0].shape
    size = shape[axis]
    place = iota(shape, axis)
    identity = (1.0, 0.0, 0.0, 1.0)
    step = 1
    while step < size:
        if direction == 1:
            keep, shift = place >= step, step
        else:
            keep, shift = place < size - step, size - step
        other = [jnp.where(keep, pltpu.roll(m, shift, axis), i) for m, i in zip(mats, identity)]
        mats = matmul2(mats, other)
        if rescale:
            factor = 1.0 / (mats[0] + mats[1] + mats[2] + mats[3])
            mats = tuple(m * factor for m in mats)
        step *= 2
    return mats


def lane(values, index):
    return jnp.broadcast_to(values[:, index : index + 1], values.shape)


def running_product(values, direction):
    size = values.shape[0]
    row = iota(values.shape, 0)
    step = 1
    while step < size:
        if direction == 1:
            keep, shift = row >= step, step
        else:
            keep, shift = row < size - step, size - step
        values = values * jnp.where(keep, pltpu.roll(values, shift, 0), 1.0)
        step *= 2
    return values


def differences(values, axis):
    size = values.shape[axis]
    place = iota(values.shape, axis)
    after = jnp.where(place == size - 1, 0.0, pltpu.roll(values, size - 1, axis))
    before = jnp.where(place == 0, 0.0, pltpu.roll(values, 1, axis))
    return after - before


def load(sources, held, arrived):
    copies = [pltpu.make_async_copy(src, dst, arrived.at[i]) for i, (src, dst) in enumerate(zip(sources, held))]
    for copy in copies:
        copy.start()
    return copies


def select_rows(row, parts):
    out = jnp.zeros(row.shape, F32)
    for index, part in enumerate(parts):
        out = jnp.where(row == index, part, out)
    return out


def sums_kernel(*refs):
    count = 11
    sources, refs = refs[:count], refs[count:]
    (own_ref, to_inner_ref, to_outer_ref, interim_ref, vectors_ref, alpha_ref, beta_ref), refs = refs[:7], refs[7:]
    held, rows_ref, arrived = refs[:count], refs[count], refs[count + 1]
    copies = load(sources, held, arrived)
    (
        weight_ref,
        height_now_ref,
        zonal_ref,
        depth_ref,
        land_ref,
        lon_ref,
        lat_ref,
        amount_ref,
        meridional_ref,
        height_old_ref,
        metric_ref,
    ) = held
    columns, rows = height_now_ref.shape
    blocks = weight_ref.shape[0]
    block = lax.axis_index("lat")
    first_east = lax.axis_index("lon") * columns
    first_north = block * rows

    copies[0].wait()
    c = 1.0 / weight_ref[...]
    one = jnp.ones_like(c)
    mats = (1.0 + c, one, c, one)
    up = product_scan(mats, 1, 1, False)
    down = product_scan(mats, 1, -1, False)
    up_all = tuple(lane(m, rows - 1) for m in up)
    down_all = tuple(lane(m, 0) for m in down)
    factor = 1.0 / (up_all[0] + up_all[1] + up_all[2] + up_all[3])
    ahead = product_scan(tuple(m * factor for m in up_all), 0, 1, True)
    factor = 1.0 / (down_all[0] + down_all[1] + down_all[2] + down_all[3])
    behind = product_scan(tuple(m * factor for m in down_all), 0, -1, True)
    row = iota(c.shape, 0)
    place = iota(c.shape, 1)
    rho = jnp.where(
        row == 0, 1.0, pltpu.roll((ahead[2] + ahead[3]) / (ahead[0] + ahead[1]), 1, 0)
    )
    sigma = jnp.where(
        row == blocks - 1,
        1.0,
        pltpu.roll((behind[2] + behind[3]) / (behind[0] + behind[1]), blocks - 1, 0),
    )
    p_after = up[0] + up[1] * rho
    q_before = down[0] + down[1] * sigma
    p = jnp.where(place == 0, 1.0, pltpu.roll(p_after, 1, 1))
    q = jnp.where(place == rows - 1, 1.0, pltpu.roll(q_before, rows - 1, 1))
    p_end = up_all[0] + up_all[1] * rho
    q_end = down_all[0] + down_all[1] * sigma
    scale = 1.0 / (up_all[2] + up_all[3] * rho + lane(p, rows - 1) * sigma)
    c_below = jnp.where(row == 0, 0.0, pltpu.roll(lane(c, rows - 1), 1, 0))
    c_above = jnp.where(row == blocks - 1, 0.0, pltpu.roll(lane(c, 0), blocks - 1, 0))
    low_p = -COURANT * c_below * (1.0 - rho)
    low_q = -COURANT * c_below * q_end
    high_p = COURANT * c_above * p_end
    high_q = COURANT * c_above * (1.0 - sigma)
    stacked = (
        p * c,
        q * c,
        q * scale,
        p * scale,
        low_p * q * scale,
        high_q * p * scale,
        jnp.where(place == 0, low_p, jnp.where(place == rows - 1, high_p, 0.0)),
        jnp.where(place == 0, low_q, jnp.where(place == rows - 1, high_q, 0.0)),
    )
    alpha_ref[...] = 1.0 / p_end
    beta_ref[...] = 1.0 / q_end
    for index, values in enumerate(stacked):
        rows_ref[index] = values
        vectors_ref[index : index + 1, :] = rows_ref[index, pl.ds(block, 1), :]

    for copy in copies[1:]:
        copy.wait()
    shape = (columns, rows)
    subs = iota(shape, 0)
    added = jnp.zeros(shape, F32)
    for chunk in range(lon_ref.shape[0]):
        amount = amount_ref[chunk : chunk + 1, :]
        here = lon_ref[chunk : chunk + 1, :] - first_east == subs
        there = jnp.where(lat_ref[chunk : chunk + 1, :] - first_north == subs, 1.0, 0.0).astype(BF16)
        for _ in range(3):
            part = amount.astype(BF16).astype(F32)
            amount = amount - part
            added += dot(jnp.where(here, part, 0.0).astype(BF16), there, (1, 1), None)

    depth = depth_ref[...] * land_ref[...].astype(F32)
    flux_east = depth * zonal_ref[...]
    flux_north = depth * meridional_ref[...]
    metric = metric_ref[...]
    interim = (
        height_old_ref[...]
        - COURANT * (metric * differences(flux_east, 0) + differences(flux_north, 1))
        + added
    )
    interim_ref[...] = interim

    eight = iota((8, rows), 0)
    along = iota((8, rows), 1)
    vectors = vectors_ref[...]
    edges = pltpu.roll(vectors, 2, 0)
    on_interim = jnp.where(eight < 2, vectors, 0.0)
    on_flux = jnp.where(eight < 2, edges, 0.0)
    on_height = jnp.where(
        ((eight == 2) & (along == rows - 1)) | ((eight == 3) & (along == 0)), 1.0, 0.0
    )
    total = dot(on_interim, interim, (1, 1)) + dot(on_flux, flux_north, (1, 1))
    total += dot(on_height, height_now_ref[...], (1, 1))
    own_ref[...] = total[0:4]

    last = columns - 1
    odd = jnp.full((8, columns), lax.axis_index("lon") & 1, jnp.int32) == 1
    line = iota((8, columns), 1)
    onto = COURANT * metric * vectors
    flux_first, flux_last = flux_east[0:1, :], flux_east[last:columns, :]
    to_west = jnp.where(line == last, -jnp.sum(onto * flux_first, axis=1, keepdims=True), 0.0)
    to_east = jnp.where(line == 0, jnp.sum(onto * flux_last, axis=1, keepdims=True), 0.0)
    to_west = jnp.where(eight < 2, to_west, jnp.where(eight == 2, height_now_ref[0:1, :], flux_first))
    to_east = jnp.where(eight < 2, to_east, jnp.where(eight == 2, height_now_ref[last:columns, :], flux_last))
    to_inner_ref[...] = jnp.where(odd, to_west, to_east)[0:4]
    to_outer_ref[...] = jnp.where(odd, to_east, to_west)[0:4]


def local_kernel(*refs):
    count = 9
    sources, refs = refs[:count], refs[count:]
    (interim_ref, vectors_ref, alpha_ref, beta_ref), refs = refs[:4], refs[4:]
    (wet_ref, zonal_part_ref, meridional_part_ref, green_ref, solved_ref, take_ref, outer_ref), refs = refs[:7], refs[7:]
    held, arrived = refs[:count], refs[count]
    copies = load(sources, held, arrived)
    (
        height_now_ref,
        zonal_ref,
        depth_ref,
        land_ref,
        meridional_ref,
        metric_ref,
        coriolis_ref,
        zonal_old_ref,
        meridional_old_ref,
    ) = held
    shape = height_now_ref.shape
    rows = shape[1]
    subs = iota(shape, 0)
    lanes = iota(shape, 1)
    blocks = alpha_ref.shape[0]
    block = lax.axis_index("lat")

    row = iota(alpha_ref.shape, 0)
    from_south = running_product(jnp.where(row < block, alpha_ref[...], 1.0), -1)
    from_north = running_product(jnp.where(row > block, beta_ref[...], 1.0), 1)
    weights = (
        jnp.where(row < block, from_south, 0.0),
        jnp.where(row > block, from_north, 0.0),
        jnp.where(row == block - 1, 1.0, 0.0),
        jnp.where(row == block + 1, 1.0, 0.0),
    )
    for source in range(blocks):
        for index, values in enumerate(weights):
            take_ref[source, index : index + 1, :] = values[source : source + 1, :]

    for copy in copies:
        copy.wait()
    wet = land_ref[...].astype(F32)
    flux_north = depth_ref[...] * wet * meridional_ref[...]

    vectors = vectors_ref[...]
    p_from = jnp.broadcast_to(vectors[0:1, :], shape).T
    q_from = jnp.broadcast_to(vectors[1:2, :], shape).T
    green = jnp.where(subs <= lanes, p_from * vectors[2:3, :], q_from * vectors[3:4, :])
    green_ref[...] = green
    solved = dot(interim_ref[...], green, (1, 0))
    solved += flux_north[:, 0:1] * vectors[4:5, :] + flux_north[:, rows - 1 : rows] * vectors[5:6, :]
    solved_ref[...] = wet * solved

    height = height_now_ref[...]
    outer_ref[...] = COURANT * metric_ref[...]
    turning = coriolis_ref[...]
    wet_ref[...] = wet
    zonal_part_ref[...] = wet * (
        zonal_old_ref[...] - COURANT * metric_ref[...] * differences(height, 0) + turning * meridional_ref[...]
    )
    meridional_part_ref[...] = wet * (
        meridional_old_ref[...] - COURANT * differences(height, 1) - turning * zonal_ref[...]
    )


def finish_kernel(
    received_ref,
    inner_ref,
    outer_ref,
    vectors_ref,
    green_ref,
    wet_ref,
    zonal_part_ref,
    meridional_part_ref,
    solved_ref,
    take_ref,
    height_ref,
    zonal_ref,
    meridional_ref,
):
    columns, rows = wet_ref.shape
    blocks = take_ref.shape[0]
    last = columns - 1
    wet = wet_ref[...]
    outer = outer_ref[...]
    eight = iota((8, rows), 0)
    along = iota((8, columns), 1)
    block = lax.axis_index("lat")
    parity = lax.axis_index("lon") & 1
    odd = jnp.full((4, columns), parity, jnp.int32) == 1
    at_own, at_other = (1 - parity) * blocks, parity * blocks

    inner = inner_ref[1 - parity]
    other = received_ref[at_other + block]
    west = jnp.where(odd, inner, other)
    east = jnp.where(odd, other, inner)
    zonal_ref[...] = zonal_part_ref[...]
    zonal_ref[0:1, :] += wet_ref[0:1, :] * outer * west[2:3, :]
    zonal_ref[last:columns, :] -= wet_ref[last:columns, :] * outer * east[2:3, :]
    halo = select_rows(eight, (0.0, 0.0, 0.0, 0.0, outer * west[3:4, :], -outer * east[3:4, :]))
    outer_rows = dot(halo, green_ref[...], (1, 0))

    sums = iota((4, columns), 0) < 2
    taken = jnp.zeros((4, columns), F32)
    for source in range(blocks):
        values = received_ref[at_own + source] + jnp.where(sums, received_ref[at_other + source], 0.0)
        taken += take_ref[source] * values
    onto = jnp.concatenate([taken, jnp.zeros_like(taken)], axis=0)
    onto = jnp.where((eight == 4) & (along == 0) | (eight == 5) & (along == last), 1.0, onto)
    heights = select_rows(
        eight, (vectors_ref[2:3, :], vectors_ref[3:4, :], 0.0, 0.0, outer_rows, outer_rows)
    )
    sides = jnp.where(
        (eight == 2) & (along == 0), COURANT, jnp.where((eight == 3) & (along == rows - 1), -COURANT, 0.0)
    )
    height_ref[...] = solved_ref[...] + wet * dot(onto, heights, (0, 0))
    meridional_ref[...] = meridional_part_ref[...] + wet * dot(onto, sides, (0, 0))


def call(kernel, outs, in_specs, scratch=()):
    return pl.pallas_call(
        kernel,
        out_shape=outs,
        in_specs=in_specs,
        out_specs=[VMEM] * len(outs),
        scratch_shapes=list(scratch),
        compiler_params=pltpu.CompilerParams(vmem_limit_bytes=LIMIT),
    )


def loading(read):
    return [pltpu.VMEM(x.shape, x.dtype) for x in read], pltpu.SemaphoreType.DMA((len(read),))


def kept(*shape):
    return pltpu.VMEM(shape, F32)


def per_device(
    height_old,
    height_now,
    zonal_old,
    zonal_now,
    meridional_old,
    meridional_now,
    ocean_depth,
    land_sea,
    metric_factor,
    coriolis,
    implicit_weight,
    source_longitude,
    source_latitude,
    source_amplitude,
):
    columns, rows = height_now.shape
    around = lax.axis_size("lon")
    blocks = lax.axis_size("lat")
    odd = lax.axis_index("lon") % 2 == 1

    def pinned(values):
        return pltpu.with_memory_space_constraint(values, pltpu.HBM)

    height_now, zonal_now, ocean_depth, land_sea, meridional_now, metric = (
        pinned(x) for x in (height_now, zonal_now, ocean_depth, land_sea, meridional_now, metric_factor[None, :])
    )
    read = (
        pinned(implicit_weight.reshape(blocks, rows)),
        height_now,
        zonal_now,
        ocean_depth,
        land_sea,
        pinned(source_longitude.reshape(-1, rows)),
        pinned(source_latitude.reshape(-1, rows)),
        pinned(source_amplitude.reshape(-1, rows)),
        meridional_now,
        pinned(height_old),
        metric,
    )
    held, arrived = loading(read)
    own, to_inner, to_outer, interim, vectors, alpha, beta = call(
        sums_kernel,
        [kept(4, columns), kept(4, columns), kept(4, columns), kept(columns, rows)]
        + [kept(8, rows), kept(blocks, rows), kept(blocks, rows)],
        [HBM] * len(read),
        [*held, pltpu.VMEM((8, blocks, rows), F32), arrived],
    )(*read)

    pairs = [[i, i + 1] for i in range(0, around, 2)]
    inner = lax.all_gather(to_inner, "lon", axis=0, axis_index_groups=pairs)
    from_inner = jnp.where(odd, inner[0], inner[1])
    own = jnp.concatenate([own[0:2] + from_inner[0:2], own[2:4]], axis=0)

    groups = [
        [lon * blocks + lat for lon in (first, (first + 1) % around) for lat in range(blocks)]
        for first in range(1, around, 2)
    ]
    parts = (blocks, 4, columns)
    low = jnp.broadcast_to(jnp.where(odd, own, to_outer), parts)
    high = jnp.broadcast_to(jnp.where(odd, to_outer, own), parts)
    received = lax.all_to_all(
        jnp.concatenate([low, high], axis=0), ("lon", "lat"), 0, 0, axis_index_groups=groups, tiled=True
    )

    read = (
        height_now,
        zonal_now,
        ocean_depth,
        land_sea,
        meridional_now,
        metric,
        pinned(coriolis[None, :]),
        pinned(zonal_old),
        pinned(meridional_old),
    )
    held, arrived = loading(read)
    wet, zonal_part, meridional_part, green, solved, take, outer = call(
        local_kernel,
        [kept(columns, rows)] * 5 + [kept(blocks, 4, rows), kept(1, rows)],
        [HBM] * len(read) + [VMEM] * 4,
        [*held, arrived],
    )(*read, interim, vectors, alpha, beta)

    block = jax.ShapeDtypeStruct((columns, rows), F32)
    return tuple(
        call(finish_kernel, [block] * 3, [VMEM] * 10)(
            received, inner, outer, vectors, green, wet, zonal_part, meridional_part, solved, take
        )
    )


def solution(mesh):
    grid = P("lon", "lat")
    placed = (grid,) * 8 + (P("lat"), P("lat"), P(), P(), P(), P())
    return jax.shard_map(
        per_device, mesh=mesh, in_specs=placed, out_specs=(grid, grid, grid), check_vma=False
    )
```

time: 40.5 us -> 31.6 us (0.78)
  the two profiles are of different devices: /device:TPU:4 before, /device:TPU:27 now
where the time goes in v3:
time: 31.6 us; the launch traced here: 31.4 us
  starting transfers between devices  13.8 us (44%)
  waiting for transfers between devices  8.68 us (27%)
  Pallas kernels  5.38 us (17%)
  blocking collectives  2.15 us (7%)
  between operations  0.68 us (2%)
  other arithmetic  0.67 us (2%)
    all_to_all x1, starting transfers between devices, per_device(): lax.all_to_all(jnp.concatenate([low, high], axis=0), ('lon', 'lat'), 0, 0...  13.8 us
    all_to_all x1, waiting for transfers between devices, per_device(): lax.all_to_all(jnp.concatenate([low, high], axis=0), ('lon', 'lat'), 0, 0...  8.68 us
    pallas_call x1, Pallas kernels, per_device(): call(sums_kernel, [kept(4, columns), kept(4, columns), kept(4, columns),...  2.8 us
    all_gather x1, blocking collectives, per_device(): inner = lax.all_gather(to_inner, 'lon', axis=0, axis_index_groups=pairs)  2.15 us
    pallas_call x1, Pallas kernels, per_device(): call(local_kernel, [kept(columns, rows)] * 5 + [kept(blocks, 4, rows), ke...  1.45 us
    pallas_call x1, Pallas kernels, per_device(): call(finish_kernel, [block] * 3, [VMEM] * 10)  1.14 us
    concatenate x1, other arithmetic, per_device(): jnp.concatenate([low, high], axis=0)  0.65 us
  transfers between devices with their start and end apart: 1, of which 1 were waited for; matrix products, arithmetic and copies ran while one was open for 0% of the time, Pallas kernels for 5%

profile of v3, /device:TPU:27, one launch (start us, length us, event | category | flops | bytes accessed | tf_op | source)
XLA Modules:
  0.0 31.4 jit_solution(12004867490768772573)
XLA Ops:
  0.6 2.8 %shard_map.157 = (f32[4,128]{1,0:T(4,128)S(1)}, f32[4,128]{1,0:T(4,128)S(1)}, f32[4,128]{1,0:T(4,128)S(1)}, f32[128,128]{1,0:T(8,128)S(1)}, f32[8,128]{1,0:T(8,1...) custom-call(f32[16,128]{1,0:T(8,128)} %bitcast.10, f32[128,128]{1,0:T(8,128)} %refs_0_.1, f32[128,128]{1,0:T(8,128)} %refs_1_.3, ...), custom_call_target="tpu_custom_call" | custom-call | tf_op jit(solution)/shard_map/pallas_call | solution.py:398
  3.4 2.2 %all-gather.1.inner_ref = f32[2,4,128]{2,1,0:T(4,128)S(1)} all-gather(f32[1,4,128]{2,1,0:T(4,128)S(1)} %bitcast.9), channel_id=2, replica_groups={{0,16},{32,48},{64,80},{96,112},{128,144},{160,176},{192,208},{224,240}..., dimensions={0}, use_global_device_ids=true | all-gather | bytes 6144 | tf_op jit(solution)/shard_map/all_gather | solution.py:407
  5.6 0.6 %pad_maximum_fusion = f32[32,4,128]{2,1,0:T(4,128)} fusion(f32[16,4,128]{2,1,0:T(4,128)S(1)} %broadcast_in_dim.14, f32[16,4,128]{2,1,0:T(4,128)S(1)} %broadcast_in_dim.13), kind=kLoop, calls=%fused_computation | loop fusion | flops 16384 | bytes 131072 | tf_op jit(solution)/shard_map/concatenate | solution.py:419
  6.3 13.8 %all-to-all-start = ((f32[32,4,128]{2,1,0:T(4,128)}), f32[32,4,128]{2,1,0:T(4,128)S(1)}, u32[]{:S(2)}, u32[]{:S(2)}) async-start(f32[32,4,128]{2,1,0:T(4,128)} %pad_maximum_fusion), calls=%async_computation | async-start | bytes 131072 | tf_op jit(solution)/shard_map/all_to_all | solution.py:418
  20.1 1.4 %shard_map.158 = (f32[128,128]{1,0:T(8,128)S(1)}, f32[128,128]{1,0:T(8,128)S(1)}, f32[128,128]{1,0:T(8,128)S(1)}, f32[128,128]{1,0:T(8,128)S(1)}, f32[128,128]{1...) custom-call(f32[128,128]{1,0:T(8,128)} %refs_0_.1, f32[128,128]{1,0:T(8,128)} %refs_1_.3, ...), custom_call_target="tpu_custom_call" | custom-call | tf_op jit(solution)/shard_map/pallas_call | solution.py:434
  21.5 8.7 %all-to-all-done.received_ref = f32[32,4,128]{2,1,0:T(4,128)S(1)} async-done(((f32[32,4,128]{2,1,0:T(4,128)}), f32[32,4,128]{2,1,0:T(4,128)S(1)}, u32[]{:S(2)}, u32[]{:S(2)}) %all-to-all-start) | async-done | bytes 65568 | tf_op jit(solution)/shard_map/all_to_all | solution.py:418
  30.2 1.1 %shard_map.159 = (f32[128,128]{1,0:T(8,128)}, f32[128,128]{1,0:T(8,128)}, f32[128,128]{1,0:T(8,128)}) custom-call(f32[32,4,128]{2,1,0:T(4,128)S(1)} %all-to-all-done.received_ref, f32[2,4,128]{2,1,0:T(4,128)S(1)} %all-gather.1.inner_ref, f32[1,128]{1,0:T(1,128)S(1)} %get-tuple-element.24.outer_ref, f32[8,128]{1,0:T(8,128)S(1)} %get-tuple-element.21.refs_10_.vectors_ref, ...), custom_call_target="tpu_custom_call" | custom-call | tf_op jit(solution)/shard_map/pallas_call | solution.py:443
  (5 shorter events, 0.0 us)
Async XLA Ops:
  6.3 23.9 %all-to-all-start = ((f32[32,4,128]{2,1,0:T(4,128)}), f32[32,4,128]{2,1,0:T(4,128)S(1)}, u32[]{:S(2)}, u32[]{:S(2)}) async-start(f32[32,4,128]{2,1,0:T(4,128)} %pad_maximum_fusion), calls=%async_computation | async-start | bytes 131072 | tf_op jit(solution)/shard_map/all_to_all | solution.py:418

commit v4 on v3

--- a/solution.py
+++ b/solution.py
@@ -37,16 +37,22 @@
     identity = (1.0, 0.0, 0.0, 1.0)
     step = 1
     while step < size:
-        if direction == 1:
-            keep, shift = place >= step, step
-        else:
-            keep, shift = place < size - step, size - step
-        other = [jnp.where(keep, pltpu.roll(m, shift, axis), i) for m, i in zip(mats, identity)]
-        mats = matmul2(mats, other)
+        reach = [step * i for i in range(1, min(4, size // step))]
+        others = []
+        for distance in reach:
+            if direction == 1:
+                keep, shift = place >= distance, distance
+            else:
+                keep, shift = place < size - distance, size - distance
+            others.append([jnp.where(keep, pltpu.roll(m, shift, axis), i) for m, i in zip(mats, identity)])
+        factors = [mats, *others]
+        while len(factors) > 1:
+            factors = [matmul2(x, y) for x, y in zip(factors[::2], factors[1::2])]
+        mats = factors[0]
         if rescale:
             factor = 1.0 / (mats[0] + mats[1] + mats[2] + mats[3])
             mats = tuple(m * factor for m in mats)
-        step *= 2
+        step *= len(reach) + 1
     return mats
 
 
@@ -87,6 +93,24 @@
     out = jnp.zeros(row.shape, F32)
     for index, part in enumerate(parts):
         out = jnp.where(row == index, part, out)
+    return out
+
+
+def thirds(values):
+    high = values.astype(BF16).astype(F32)
+    rest = values - high
+    middle = rest.astype(BF16).astype(F32)
+    return high, middle, rest - middle
+
+
+def sums_dot(a, b):
+    size = a.shape[0]
+    left = jnp.concatenate(thirds(a), axis=0).astype(BF16)
+    out = jnp.zeros((size, b.shape[0]), F32)
+    for skip, part in enumerate(thirds(b)):
+        product = dot(left, part.astype(BF16), (1, 1), None)
+        for index in range(3 - skip):
+            out += product[index * size : (index + 1) * size]
     return out
 
 
@@ -115,7 +139,8 @@
     first_east = lax.axis_index("lon") * columns
     first_north = block * rows
 
-    copies[0].wait()
+    for copy in copies:
+        copy.wait()
     c = 1.0 / weight_ref[...]
     one = jnp.ones_like(c)
     mats = (1.0 + c, one, c, one)
@@ -166,19 +191,18 @@
         rows_ref[index] = values
         vectors_ref[index : index + 1, :] = rows_ref[index, pl.ds(block, 1), :]
 
-    for copy in copies[1:]:
-        copy.wait()
     shape = (columns, rows)
     subs = iota(shape, 0)
     added = jnp.zeros(shape, F32)
-    for chunk in range(lon_ref.shape[0]):
-        amount = amount_ref[chunk : chunk + 1, :]
-        here = lon_ref[chunk : chunk + 1, :] - first_east == subs
-        there = jnp.where(lat_ref[chunk : chunk + 1, :] - first_north == subs, 1.0, 0.0).astype(BF16)
-        for _ in range(3):
-            part = amount.astype(BF16).astype(F32)
-            amount = amount - part
-            added += dot(jnp.where(here, part, 0.0).astype(BF16), there, (1, 1), None)
+    parts = thirds(amount_ref[...])
+    chunks = range(lon_ref.shape[0])
+    here = [lon_ref[i : i + 1, :] - first_east == subs for i in chunks]
+    there = jnp.concatenate(
+        [jnp.where(lat_ref[i : i + 1, :] - first_north == subs, 1.0, 0.0) for i in chunks], axis=1
+    ).astype(BF16)
+    for part in parts:
+        amounts = jnp.concatenate([jnp.where(here[i], part[i : i + 1, :], 0.0) for i in chunks], axis=1)
+        added += dot(amounts.astype(BF16), there, (1, 1), None)
 
     depth = depth_ref[...] * land_ref[...].astype(F32)
     flux_east = depth * zonal_ref[...]
@@ -194,14 +218,14 @@
     eight = iota((8, rows), 0)
     along = iota((8, rows), 1)
     vectors = vectors_ref[...]
-    edges = pltpu.roll(vectors, 2, 0)
     on_interim = jnp.where(eight < 2, vectors, 0.0)
-    on_flux = jnp.where(eight < 2, edges, 0.0)
-    on_height = jnp.where(
-        ((eight == 2) & (along == rows - 1)) | ((eight == 3) & (along == 0)), 1.0, 0.0
-    )
-    total = dot(on_interim, interim, (1, 1)) + dot(on_flux, flux_north, (1, 1))
-    total += dot(on_height, height_now_ref[...], (1, 1))
+    on_edges = jnp.where(eight < 2, pltpu.roll(vectors, 2, 0), 0.0)
+    on_edges += jnp.where((eight == 2) & (along == 1) | (eight == 3) & (along == 2), 1.0, 0.0)
+    lanes = iota(shape, 1)
+    edges = jnp.where((lanes == 0) | (lanes == rows - 1), flux_north, pltpu.roll(height_now_ref[...], 2, 1))
+    total = sums_dot(
+        jnp.concatenate([on_interim, on_edges], axis=1), jnp.concatenate([interim, edges], axis=1)
+    )
     own_ref[...] = total[0:4]
 
     last = columns - 1
@@ -215,6 +239,26 @@
     to_east = jnp.where(eight < 2, to_east, jnp.where(eight == 2, height_now_ref[last:columns, :], flux_last))
     to_inner_ref[...] = jnp.where(odd, to_west, to_east)[0:4]
     to_outer_ref[...] = jnp.where(odd, to_east, to_west)[0:4]
+
+
+def pack_kernel(own_ref, inner_ref, to_outer_ref, send_ref):
+    blocks = send_ref.shape[0] // 2
+    block = lax.axis_index("lat")
+    parity = lax.axis_index("lon") & 1
+    at_own, at_outer = (1 - parity) * blocks, parity * blocks
+    own = own_ref[...]
+    row = iota(own.shape, 0)
+    own += jnp.where(row < 2, inner_ref[1 - parity], 0.0)
+    outer = to_outer_ref[...]
+    own_up = jnp.concatenate([own[0:1], own[2:3]], axis=0)
+    own_down = jnp.concatenate([own[1:2], own[3:4]], axis=0)
+    outer_up = jnp.concatenate([outer[0:1], jnp.zeros_like(outer[0:1])], axis=0)
+    outer_down = jnp.concatenate([outer[1:2], jnp.zeros_like(outer[0:1])], axis=0)
+    for target in range(blocks):
+        north = jnp.full(own_up.shape, (block < target).astype(jnp.int32), jnp.int32) == 1
+        send_ref[at_own + target] = jnp.where(north, own_up, own_down)
+        send_ref[at_outer + target] = jnp.where(north, outer_up, outer_down)
+    send_ref[at_outer + block] = outer[2:4]
 
 
 def local_kernel(*refs):
@@ -247,8 +291,8 @@
     from_north = running_product(jnp.where(row > block, beta_ref[...], 1.0), 1)
     weights = (
         jnp.where(row < block, from_south, 0.0),
+        jnp.where(row == block - 1, 1.0, 0.0),
         jnp.where(row > block, from_north, 0.0),
-        jnp.where(row == block - 1, 1.0, 0.0),
         jnp.where(row == block + 1, 1.0, 0.0),
     )
     for source in range(blocks):
@@ -264,7 +308,8 @@
     p_from = jnp.broadcast_to(vectors[0:1, :], shape).T
     q_from = jnp.broadcast_to(vectors[1:2, :], shape).T
     green = jnp.where(subs <= lanes, p_from * vectors[2:3, :], q_from * vectors[3:4, :])
-    green_ref[...] = green
+    for index, part in enumerate(thirds(green)):
+        green_ref[index] = part.astype(BF16)
     solved = dot(interim_ref[...], green, (1, 0))
     solved += flux_north[:, 0:1] * vectors[4:5, :] + flux_north[:, rows - 1 : rows] * vectors[5:6, :]
     solved_ref[...] = wet * solved
@@ -305,34 +350,51 @@
     along = iota((8, columns), 1)
     block = lax.axis_index("lat")
     parity = lax.axis_index("lon") & 1
-    odd = jnp.full((4, columns), parity, jnp.int32) == 1
     at_own, at_other = (1 - parity) * blocks, parity * blocks
 
-    inner = inner_ref[1 - parity]
+    inner = inner_ref[1 - parity][2:4]
     other = received_ref[at_other + block]
+    odd = jnp.full(other.shape, parity, jnp.int32) == 1
     west = jnp.where(odd, inner, other)
     east = jnp.where(odd, other, inner)
     zonal_ref[...] = zonal_part_ref[...]
-    zonal_ref[0:1, :] += wet_ref[0:1, :] * outer * west[2:3, :]
-    zonal_ref[last:columns, :] -= wet_ref[last:columns, :] * outer * east[2:3, :]
-    halo = select_rows(eight, (0.0, 0.0, 0.0, 0.0, outer * west[3:4, :], -outer * east[3:4, :]))
-    outer_rows = dot(halo, green_ref[...], (1, 0))
-
-    sums = iota((4, columns), 0) < 2
-    taken = jnp.zeros((4, columns), F32)
+    zonal_ref[0:1, :] += wet_ref[0:1, :] * outer * west[0:1, :]
+    zonal_ref[last:columns, :] -= wet_ref[last:columns, :] * outer * east[0:1, :]
+
+    halo = select_rows(eight, (0.0, 0.0, 0.0, 0.0, outer * west[1:2, :], -outer * east[1:2, :]))
+    left = jnp.concatenate(thirds(halo), axis=0).astype(BF16)
+    outer_rows = jnp.zeros((8, rows), F32)
+    for skip in range(3):
+        product = dot(left, green_ref[skip], (1, 0), None)
+        for index in range(3 - skip):
+            outer_rows += product[8 * index : 8 * index + 8]
+
+    south = jnp.zeros(other.shape, F32)
+    north = jnp.zeros(other.shape, F32)
     for source in range(blocks):
-        values = received_ref[at_own + source] + jnp.where(sums, received_ref[at_other + source], 0.0)
-        taken += take_ref[source] * values
-    onto = jnp.concatenate([taken, jnp.zeros_like(taken)], axis=0)
+        values = received_ref[at_own + source] + received_ref[at_other + source]
+        take = take_ref[source]
+        south += take[0:2] * values
+        north += take[2:4] * values
+    onto = jnp.concatenate([south, north, jnp.zeros((4, columns), F32)], axis=0)
     onto = jnp.where((eight == 4) & (along == 0) | (eight == 5) & (along == last), 1.0, onto)
     heights = select_rows(
-        eight, (vectors_ref[2:3, :], vectors_ref[3:4, :], 0.0, 0.0, outer_rows, outer_rows)
+        eight, (vectors_ref[2:3, :], 0.0, vectors_ref[3:4, :], 0.0, outer_rows, outer_rows)
     )
     sides = jnp.where(
-        (eight == 2) & (along == 0), COURANT, jnp.where((eight == 3) & (along == rows - 1), -COURANT, 0.0)
-    )
-    height_ref[...] = solved_ref[...] + wet * dot(onto, heights, (0, 0))
-    meridional_ref[...] = meridional_part_ref[...] + wet * dot(onto, sides, (0, 0))
+        (eight == 1) & (along == 0), COURANT, jnp.where((eight == 3) & (along == rows - 1), -COURANT, 0.0)
+    )
+    left = thirds(onto)
+    right = thirds(jnp.concatenate([heights, sides], axis=1))
+    pairs = [(i, j) for i in range(3) for j in range(3 - i)]
+    both = dot(
+        jnp.concatenate([left[i] for i, _ in pairs], axis=0).astype(BF16),
+        jnp.concatenate([right[j] for _, j in pairs], axis=0).astype(BF16),
+        (0, 0),
+        None,
+    )
+    height_ref[...] = solved_ref[...] + wet * both[:, :rows]
+    meridional_ref[...] = meridional_part_ref[...] + wet * both[:, rows:]
 
 
 def call(kernel, outs, in_specs, scratch=()):
@@ -373,7 +435,6 @@
     columns, rows = height_now.shape
     around = lax.axis_size("lon")
     blocks = lax.axis_size("lat")
-    odd = lax.axis_index("lon") % 2 == 1
 
     def pinned(values):
         return pltpu.with_memory_space_constraint(values, pltpu.HBM)
@@ -405,19 +466,13 @@
 
     pairs = [[i, i + 1] for i in range(0, around, 2)]
     inner = lax.all_gather(to_inner, "lon", axis=0, axis_index_groups=pairs)
-    from_inner = jnp.where(odd, inner[0], inner[1])
-    own = jnp.concatenate([own[0:2] + from_inner[0:2], own[2:4]], axis=0)
 
     groups = [
         [lon * blocks + lat for lon in (first, (first + 1) % around) for lat in range(blocks)]
         for first in range(1, around, 2)
     ]
-    parts = (blocks, 4, columns)
-    low = jnp.broadcast_to(jnp.where(odd, own, to_outer), parts)
-    high = jnp.broadcast_to(jnp.where(odd, to_outer, own), parts)
-    received = lax.all_to_all(
-        jnp.concatenate([low, high], axis=0), ("lon", "lat"), 0, 0, axis_index_groups=groups, tiled=True
-    )
+    (send,) = call(pack_kernel, [kept(2 * blocks, 2, columns)], [VMEM] * 3)(own, inner, to_outer)
+    received = lax.all_to_all(send, ("lon", "lat"), 0, 0, axis_index_groups=groups, tiled=True)
 
     read = (
         height_now,
@@ -433,7 +488,8 @@
     held, arrived = loading(read)
     wet, zonal_part, meridional_part, green, solved, take, outer = call(
         local_kernel,
-        [kept(columns, rows)] * 5 + [kept(blocks, 4, rows), kept(1, rows)],
+        [kept(columns, rows)] * 3
+        + [pltpu.VMEM((3, rows, rows), BF16), kept(columns, rows), kept(blocks, 4, rows), kept(1, rows)],
         [HBM] * len(read) + [VMEM] * 4,
         [*held, arrived],
     )(*read, interim, vectors, alpha, beta)

time: 31.6 us -> 30.5 us (0.965)
  other arithmetic: 0.67 us -> 0 us
    pallas_call x1, Pallas kernels: 2.8 us -> 2.06 us  [per_device(): call(sums_kernel, [kept(4, columns), kept(4, columns), kept(4, columns),...]
    concatenate x1 -> x0, other arithmetic: 0.65 us -> none  [per_device(): jnp.concatenate([low, high], axis=0)]
    pallas_call x1 -> x2, Pallas kernels: 1.45 us -> 2.09 us  [the longest x1 1.45 us: per_device(): call(local_kernel, [kept(columns, rows)] * 3 + [pltpu.VMEM((3, rows, rows...]
where the time goes in v4:
time: 30.5 us; the launch traced here: 30.2 us
  starting transfers between devices  13.8 us (45%)
  waiting for transfers between devices  8.51 us (28%)
  Pallas kernels  5.12 us (17%)
  blocking collectives  2.15 us (7%)
  between operations  0.66 us (2%)
    all_to_all x1, starting transfers between devices, per_device(): lax.all_to_all(send, ('lon', 'lat'), 0, 0, axis_index_groups=groups, tile...  13.8 us
    all_to_all x1, waiting for transfers between devices, per_device(): lax.all_to_all(send, ('lon', 'lat'), 0, 0, axis_index_groups=groups, tile...  8.51 us
    all_gather x1, blocking collectives, per_device(): inner = lax.all_gather(to_inner, 'lon', axis=0, axis_index_groups=pairs)  2.15 us
    pallas_call x1, Pallas kernels, per_device(): call(sums_kernel, [kept(4, columns), kept(4, columns), kept(4, columns),...  2.06 us
    pallas_call x1, Pallas kernels, per_device(): call(local_kernel, [kept(columns, rows)] * 3 + [pltpu.VMEM((3, rows, rows...  1.45 us
    pallas_call x1, Pallas kernels, per_device(): call(finish_kernel, [block] * 3, [VMEM] * 10)  0.98 us
    pallas_call x1, Pallas kernels, per_device(): call(pack_kernel, [kept(2 * blocks, 2, columns)], [VMEM] * 3)  0.64 us
  transfers between devices with their start and end apart: 1, of which 1 were waited for; matrix products, arithmetic and copies ran while one was open for 0% of the time, Pallas kernels for 5%

profile of v4, /device:TPU:27, one launch (start us, length us, event | category | flops | bytes accessed | tf_op | source)
XLA Modules:
  0.0 30.2 jit_solution(7467719532290981879)
XLA Ops:
  0.6 2.1 %shard_map.157 = (f32[4,128]{1,0:T(4,128)S(1)}, f32[4,128]{1,0:T(4,128)S(1)}, f32[4,128]{1,0:T(4,128)S(1)}, f32[128,128]{1,0:T(8,128)S(1)}, f32[8,128]{1,0:T(8,1...) custom-call(f32[16,128]{1,0:T(8,128)} %bitcast.8, f32[128,128]{1,0:T(8,128)} %refs_0_.1, f32[128,128]{1,0:T(8,128)} %refs_1_.3, ...), custom_call_target="tpu_custom_call" | custom-call | tf_op jit(solution)/shard_map/pallas_call | solution.py:459
  2.7 2.2 %all-gather.1.inner_ref = f32[2,4,128]{2,1,0:T(4,128)S(1)} all-gather(f32[1,4,128]{2,1,0:T(4,128)S(1)} %bitcast.7), channel_id=2, replica_groups={{0,16},{32,48},{64,80},{96,112},{128,144},{160,176},{192,208},{224,240}..., dimensions={0}, use_global_device_ids=true | all-gather | bytes 6144 | tf_op jit(solution)/shard_map/all_gather | solution.py:468
  4.8 0.6 %shard_map.158 = f32[32,2,128]{2,1,0:T(2,128)} custom-call(f32[4,128]{1,0:T(4,128)S(1)} %get-tuple-element.17.own_ref, f32[2,4,128]{2,1,0:T(4,128)S(1)} %all-gather.1.inner_ref, f32[4,128]{1,0:T(4,128)S(1)} %get-tuple-element.19.to_outer_ref), custom_call_target="tpu_custom_call" | custom-call | tf_op jit(solution)/shard_map/pallas_call | solution.py:474
  5.5 13.8 %all-to-all-start = ((f32[32,2,128]{2,1,0:T(2,128)}), f32[32,2,128]{2,1,0:T(2,128)S(1)}, u32[]{:S(2)}, u32[]{:S(2)}) async-start(f32[32,2,128]{2,1,0:T(2,128)} %shard_map.158), calls=%async_computation | async-start | bytes 65536 | tf_op jit(solution)/shard_map/all_to_all | solution.py:475
  19.3 1.5 %shard_map.159 = (f32[128,128]{1,0:T(8,128)S(1)}, f32[128,128]{1,0:T(8,128)S(1)}, f32[128,128]{1,0:T(8,128)S(1)}, bf16[3,128,128]{2,1,0:T(8,128)(2,1)S(1)}, f32[...) custom-call(f32[128,128]{1,0:T(8,128)} %refs_0_.1, f32[128,128]{1,0:T(8,128)} %refs_1_.3, ...), custom_call_target="tpu_custom_call" | custom-call | tf_op jit(solution)/shard_map/pallas_call | solution.py:489
  20.7 8.5 %all-to-all-done.received_ref = f32[32,2,128]{2,1,0:T(2,128)S(1)} async-done(((f32[32,2,128]{2,1,0:T(2,128)}), f32[32,2,128]{2,1,0:T(2,128)S(1)}, u32[]{:S(2)}, u32[]{:S(2)}) %all-to-all-start) | async-done | bytes 32800 | tf_op jit(solution)/shard_map/all_to_all | solution.py:475
  29.2 1.0 %shard_map.160 = (f32[128,128]{1,0:T(8,128)}, f32[128,128]{1,0:T(8,128)}, f32[128,128]{1,0:T(8,128)}) custom-call(f32[32,2,128]{2,1,0:T(2,128)S(1)} %all-to-all-done.received_ref, f32[2,4,128]{2,1,0:T(4,128)S(1)} %all-gather.1.inner_ref, f32[1,128]{1,0:T(1,128)S(1)} %get-tuple-element.24.outer_ref, f32[8,128]{1,0:T(8,128)S(1)} %get-tuple-element.21.refs_10_.vectors_ref, ...), custom_call_target="tpu_custom_call" | custom-call | tf_op jit(solution)/shard_map/pallas_call | solution.py:499
Async XLA Ops:
  5.5 23.7 %all-to-all-start = ((f32[32,2,128]{2,1,0:T(2,128)}), f32[32,2,128]{2,1,0:T(2,128)S(1)}, u32[]{:S(2)}, u32[]{:S(2)}) async-start(f32[32,2,128]{2,1,0:T(2,128)} %shard_map.158), calls=%async_computation | async-start | bytes 65536 | tf_op jit(solution)/shard_map/all_to_all | solution.py:475

commit v5 on v4

--- a/solution.py
+++ b/solution.py
@@ -245,7 +245,7 @@
     blocks = send_ref.shape[0] // 2
     block = lax.axis_index("lat")
     parity = lax.axis_index("lon") & 1
-    at_own, at_outer = (1 - parity) * blocks, parity * blocks
+    at_own, at_outer = parity * blocks, (1 - parity) * blocks
     own = own_ref[...]
     row = iota(own.shape, 0)
     own += jnp.where(row < 2, inner_ref[1 - parity], 0.0)
@@ -256,9 +256,10 @@
     outer_down = jnp.concatenate([outer[1:2], jnp.zeros_like(outer[0:1])], axis=0)
     for target in range(blocks):
         north = jnp.full(own_up.shape, (block < target).astype(jnp.int32), jnp.int32) == 1
-        send_ref[at_own + target] = jnp.where(north, own_up, own_down)
-        send_ref[at_outer + target] = jnp.where(north, outer_up, outer_down)
-    send_ref[at_outer + block] = outer[2:4]
+        slot = blocks - 1 - target
+        send_ref[at_own + slot] = jnp.where(north, own_up, own_down)
+        send_ref[at_outer + slot] = jnp.where(north, outer_up, outer_down)
+    send_ref[at_outer + blocks - 1 - block] = outer[2:4]
 
 
 def local_kernel(*refs):
@@ -350,10 +351,10 @@
     along = iota((8, columns), 1)
     block = lax.axis_index("lat")
     parity = lax.axis_index("lon") & 1
-    at_own, at_other = (1 - parity) * blocks, parity * blocks
+    at_own, at_other = parity * blocks, (1 - parity) * blocks
 
     inner = inner_ref[1 - parity][2:4]
-    other = received_ref[at_other + block]
+    other = received_ref[at_other + blocks - 1 - block]
     odd = jnp.full(other.shape, parity, jnp.int32) == 1
     west = jnp.where(odd, inner, other)
     east = jnp.where(odd, other, inner)
@@ -372,7 +373,8 @@
     south = jnp.zeros(other.shape, F32)
     north = jnp.zeros(other.shape, F32)
     for source in range(blocks):
-        values = received_ref[at_own + source] + received_ref[at_other + source]
+        slot = blocks - 1 - source
+        values = received_ref[at_own + slot] + received_ref[at_other + slot]
         take = take_ref[source]
         south += take[0:2] * values
         north += take[2:4] * values
@@ -468,7 +470,7 @@
     inner = lax.all_gather(to_inner, "lon", axis=0, axis_index_groups=pairs)
 
     groups = [
-        [lon * blocks + lat for lon in (first, (first + 1) % around) for lat in range(blocks)]
+        [lon * blocks + lat for lon in ((first + 1) % around, first) for lat in reversed(range(blocks))]
         for first in range(1, around, 2)
     ]
     (send,) = call(pack_kernel, [kept(2 * blocks, 2, columns)], [VMEM] * 3)(own, inner, to_outer)

time: 30.5 us -> 28.6 us (0.938)
  the two profiles are of different devices: /device:TPU:27 before, /device:TPU:31 now
where the time goes in v5:
time: 28.6 us; the launch traced here: 28.4 us
  starting transfers between devices  15.1 us (53%)
  waiting for transfers between devices  5.28 us (18%)
  Pallas kernels  5.13 us (18%)
  blocking collectives  2.15 us (8%)
  between operations  0.66 us (2%)
    all_to_all x1, starting transfers between devices, per_device(): lax.all_to_all(send, ('lon', 'lat'), 0, 0, axis_index_groups=groups, tile...  15.1 us
    all_to_all x1, waiting for transfers between devices, per_device(): lax.all_to_all(send, ('lon', 'lat'), 0, 0, axis_index_groups=groups, tile...  5.28 us
    all_gather x1, blocking collectives, per_device(): inner = lax.all_gather(to_inner, 'lon', axis=0, axis_index_groups=pairs)  2.15 us
    pallas_call x1, Pallas kernels, per_device(): call(sums_kernel, [kept(4, columns), kept(4, columns), kept(4, columns),...  2.06 us
    pallas_call x1, Pallas kernels, per_device(): call(local_kernel, [kept(columns, rows)] * 3 + [pltpu.VMEM((3, rows, rows...  1.45 us
    pallas_call x1, Pallas kernels, per_device(): call(finish_kernel, [block] * 3, [VMEM] * 10)  0.98 us
    pallas_call x1, Pallas kernels, per_device(): call(pack_kernel, [kept(2 * blocks, 2, columns)], [VMEM] * 3)  0.64 us
  transfers between devices with their start and end apart: 1, of which 1 were waited for; matrix products, arithmetic and copies ran while one was open for 0% of the time, Pallas kernels for 5%

profile of v5, /device:TPU:31, one launch (start us, length us, event | category | flops | bytes accessed | tf_op | source)
XLA Modules:
  0.0 28.4 jit_solution(2606274096250186368)
XLA Ops:
  0.6 2.1 %shard_map.157 = (f32[4,128]{1,0:T(4,128)S(1)}, f32[4,128]{1,0:T(4,128)S(1)}, f32[4,128]{1,0:T(4,128)S(1)}, f32[128,128]{1,0:T(8,128)S(1)}, f32[8,128]{1,0:T(8,1...) custom-call(f32[16,128]{1,0:T(8,128)} %bitcast.8, f32[128,128]{1,0:T(8,128)} %refs_0_.1, f32[128,128]{1,0:T(8,128)} %refs_1_.3, ...), custom_call_target="tpu_custom_call" | custom-call | tf_op jit(solution)/shard_map/pallas_call | solution.py:461
  2.7 2.2 %all-gather.1.inner_ref = f32[2,4,128]{2,1,0:T(4,128)S(1)} all-gather(f32[1,4,128]{2,1,0:T(4,128)S(1)} %bitcast.7), channel_id=2, replica_groups={{0,16},{32,48},{64,80},{96,112},{128,144},{160,176},{192,208},{224,240}..., dimensions={0}, use_global_device_ids=true | all-gather | bytes 6144 | tf_op jit(solution)/shard_map/all_gather | solution.py:470
  4.9 0.6 %shard_map.158 = f32[32,2,128]{2,1,0:T(2,128)} custom-call(f32[4,128]{1,0:T(4,128)S(1)} %get-tuple-element.17.own_ref, f32[2,4,128]{2,1,0:T(4,128)S(1)} %all-gather.1.inner_ref, f32[4,128]{1,0:T(4,128)S(1)} %get-tuple-element.19.to_outer_ref), custom_call_target="tpu_custom_call" | custom-call | tf_op jit(solution)/shard_map/pallas_call | solution.py:476
  5.5 15.1 %all-to-all-start = ((f32[32,2,128]{2,1,0:T(2,128)}), f32[32,2,128]{2,1,0:T(2,128)S(1)}, u32[]{:S(2)}, u32[]{:S(2)}) async-start(f32[32,2,128]{2,1,0:T(2,128)} %shard_map.158), calls=%async_computation | async-start | bytes 65536 | tf_op jit(solution)/shard_map/all_to_all | solution.py:477
  20.6 1.5 %shard_map.159 = (f32[128,128]{1,0:T(8,128)S(1)}, f32[128,128]{1,0:T(8,128)S(1)}, f32[128,128]{1,0:T(8,128)S(1)}, bf16[3,128,128]{2,1,0:T(8,128)(2,1)S(1)}, f32[...) custom-call(f32[128,128]{1,0:T(8,128)} %refs_0_.1, f32[128,128]{1,0:T(8,128)} %refs_1_.3, ...), custom_call_target="tpu_custom_call" | custom-call | tf_op jit(solution)/shard_map/pallas_call | solution.py:491
  22.1 5.3 %all-to-all-done.received_ref = f32[32,2,128]{2,1,0:T(2,128)S(1)} async-done(((f32[32,2,128]{2,1,0:T(2,128)}), f32[32,2,128]{2,1,0:T(2,128)S(1)}, u32[]{:S(2)}, u32[]{:S(2)}) %all-to-all-start) | async-done | bytes 32800 | tf_op jit(solution)/shard_map/all_to_all | solution.py:477
  27.4 1.0 %shard_map.160 = (f32[128,128]{1,0:T(8,128)}, f32[128,128]{1,0:T(8,128)}, f32[128,128]{1,0:T(8,128)}) custom-call(f32[32,2,128]{2,1,0:T(2,128)S(1)} %all-to-all-done.received_ref, f32[2,4,128]{2,1,0:T(4,128)S(1)} %all-gather.1.inner_ref, f32[1,128]{1,0:T(1,128)S(1)} %get-tuple-element.24.outer_ref, f32[8,128]{1,0:T(8,128)S(1)} %get-tuple-element.21.refs_10_.vectors_ref, ...), custom_call_target="tpu_custom_call" | custom-call | tf_op jit(solution)/shard_map/pallas_call | solution.py:501
Async XLA Ops:
  5.5 21.9 %all-to-all-start = ((f32[32,2,128]{2,1,0:T(2,128)}), f32[32,2,128]{2,1,0:T(2,128)S(1)}, u32[]{:S(2)}, u32[]{:S(2)}) async-start(f32[32,2,128]{2,1,0:T(2,128)} %shard_map.158), calls=%async_computation | async-start | bytes 65536 | tf_op jit(solution)/shard_map/all_to_all | solution.py:477

commit v6 on v4

--- a/solution.py
+++ b/solution.py
@@ -82,6 +82,13 @@
     return after - before
 
 
+def place(lat, blocks):
+    half = blocks // 2
+    if isinstance(lat, int):
+        return blocks - 1 - lat if lat >= half else half + lat
+    return jnp.where(lat >= half, blocks - 1 - lat, half + lat)
+
+
 def load(sources, held, arrived):
     copies = [pltpu.make_async_copy(src, dst, arrived.at[i]) for i, (src, dst) in enumerate(zip(sources, held))]
     for copy in copies:
@@ -245,7 +252,6 @@
     blocks = send_ref.shape[0] // 2
     block = lax.axis_index("lat")
     parity = lax.axis_index("lon") & 1
-    at_own, at_outer = (1 - parity) * blocks, parity * blocks
     own = own_ref[...]
     row = iota(own.shape, 0)
     own += jnp.where(row < 2, inner_ref[1 - parity], 0.0)
@@ -256,9 +262,10 @@
     outer_down = jnp.concatenate([outer[1:2], jnp.zeros_like(outer[0:1])], axis=0)
     for target in range(blocks):
         north = jnp.full(own_up.shape, (block < target).astype(jnp.int32), jnp.int32) == 1
-        send_ref[at_own + target] = jnp.where(north, own_up, own_down)
-        send_ref[at_outer + target] = jnp.where(north, outer_up, outer_down)
-    send_ref[at_outer + block] = outer[2:4]
+        slot = 2 * place(target, blocks)
+        send_ref[slot + parity] = jnp.where(north, own_up, own_down)
+        send_ref[slot + 1 - parity] = jnp.where(north, outer_up, outer_down)
+    send_ref[2 * place(block, blocks) + 1 - parity] = outer[2:4]
 
 
 def local_kernel(*refs):
@@ -350,10 +357,9 @@
     along = iota((8, columns), 1)
     block = lax.axis_index("lat")
     parity = lax.axis_index("lon") & 1
-    at_own, at_other = (1 - parity) * blocks, parity * blocks
 
     inner = inner_ref[1 - parity][2:4]
-    other = received_ref[at_other + block]
+    other = received_ref[2 * place(block, blocks) + 1 - parity]
     odd = jnp.full(other.shape, parity, jnp.int32) == 1
     west = jnp.where(odd, inner, other)
     east = jnp.where(odd, other, inner)
@@ -372,7 +378,8 @@
     south = jnp.zeros(other.shape, F32)
     north = jnp.zeros(other.shape, F32)
     for source in range(blocks):
-        values = received_ref[at_own + source] + received_ref[at_other + source]
+        slot = 2 * place(source, blocks)
+        values = received_ref[slot] + received_ref[slot + 1]
         take = take_ref[source]
         south += take[0:2] * values
         north += take[2:4] * values
@@ -467,8 +474,9 @@
     pairs = [[i, i + 1] for i in range(0, around, 2)]
     inner = lax.all_gather(to_inner, "lon", axis=0, axis_index_groups=pairs)
 
+    order = sorted(range(blocks), key=lambda lat: place(lat, blocks))
     groups = [
-        [lon * blocks + lat for lon in (first, (first + 1) % around) for lat in range(blocks)]
+        [lon * blocks + lat for lat in order for lon in ((first + 1) % around, first)]
         for first in range(1, around, 2)
     ]
     (send,) = call(pack_kernel, [kept(2 * blocks, 2, columns)], [VMEM] * 3)(own, inner, to_outer)

time: 30.5 us -> 28.8 us (0.944)
  waiting for transfers between devices: 8.51 us -> 4.88 us
  starting transfers between devices: 13.8 us -> 15.7 us
    all_to_all x1, waiting for transfers between devices: 8.51 us -> 4.88 us  [per_device(): lax.all_to_all(send, ('lon', 'lat'), 0, 0, axis_index_groups=groups, tile...]
    all_to_all x1, starting transfers between devices: 13.8 us -> 15.7 us  [per_device(): lax.all_to_all(send, ('lon', 'lat'), 0, 0, axis_index_groups=groups, tile...]
where the time goes in v6:
time: 28.8 us; the launch traced here: 28.5 us
  starting transfers between devices  15.7 us (55%)
  Pallas kernels  5.13 us (18%)
  waiting for transfers between devices  4.88 us (17%)
  blocking collectives  2.15 us (7%)
  between operations  0.66 us (2%)
    all_to_all x1, starting transfers between devices, per_device(): lax.all_to_all(send, ('lon', 'lat'), 0, 0, axis_index_groups=groups, tile...  15.7 us
    all_to_all x1, waiting for transfers between devices, per_device(): lax.all_to_all(send, ('lon', 'lat'), 0, 0, axis_index_groups=groups, tile...  4.88 us
    all_gather x1, blocking collectives, per_device(): inner = lax.all_gather(to_inner, 'lon', axis=0, axis_index_groups=pairs)  2.15 us
    pallas_call x1, Pallas kernels, per_device(): call(sums_kernel, [kept(4, columns), kept(4, columns), kept(4, columns),...  2.06 us
    pallas_call x1, Pallas kernels, per_device(): call(local_kernel, [kept(columns, rows)] * 3 + [pltpu.VMEM((3, rows, rows...  1.45 us
    pallas_call x1, Pallas kernels, per_device(): call(finish_kernel, [block] * 3, [VMEM] * 10)  0.97 us
    pallas_call x1, Pallas kernels, per_device(): call(pack_kernel, [kept(2 * blocks, 2, columns)], [VMEM] * 3)  0.64 us
  transfers between devices with their start and end apart: 1, of which 1 were waited for; matrix products, arithmetic and copies ran while one was open for 0% of the time, Pallas kernels for 5%

profile of v6, /device:TPU:27, one launch (start us, length us, event | category | flops | bytes accessed | tf_op | source)
XLA Modules:
  0.0 28.5 jit_solution(594616069798895724)
XLA Ops:
  0.6 2.1 %shard_map.157 = (f32[4,128]{1,0:T(4,128)S(1)}, f32[4,128]{1,0:T(4,128)S(1)}, f32[4,128]{1,0:T(4,128)S(1)}, f32[128,128]{1,0:T(8,128)S(1)}, f32[8,128]{1,0:T(8,1...) custom-call(f32[16,128]{1,0:T(8,128)} %bitcast.8, f32[128,128]{1,0:T(8,128)} %refs_0_.1, f32[128,128]{1,0:T(8,128)} %refs_1_.3, ...), custom_call_target="tpu_custom_call" | custom-call | tf_op jit(solution)/shard_map/pallas_call | solution.py:466
  2.7 2.2 %all-gather.1.inner_ref = f32[2,4,128]{2,1,0:T(4,128)S(1)} all-gather(f32[1,4,128]{2,1,0:T(4,128)S(1)} %bitcast.7), channel_id=2, replica_groups={{0,16},{32,48},{64,80},{96,112},{128,144},{160,176},{192,208},{224,240}..., dimensions={0}, use_global_device_ids=true | all-gather | bytes 6144 | tf_op jit(solution)/shard_map/all_gather | solution.py:475
  4.8 0.6 %shard_map.158 = f32[32,2,128]{2,1,0:T(2,128)} custom-call(f32[4,128]{1,0:T(4,128)S(1)} %get-tuple-element.17.own_ref, f32[2,4,128]{2,1,0:T(4,128)S(1)} %all-gather.1.inner_ref, f32[4,128]{1,0:T(4,128)S(1)} %get-tuple-element.19.to_outer_ref), custom_call_target="tpu_custom_call" | custom-call | tf_op jit(solution)/shard_map/pallas_call | solution.py:482
  5.5 15.7 %all-to-all-start = ((f32[32,2,128]{2,1,0:T(2,128)}), f32[32,2,128]{2,1,0:T(2,128)S(1)}, u32[]{:S(2)}, u32[]{:S(2)}) async-start(f32[32,2,128]{2,1,0:T(2,128)} %shard_map.158), calls=%async_computation | async-start | bytes 65536 | tf_op jit(solution)/shard_map/all_to_all | solution.py:483
  21.2 1.5 %shard_map.159 = (f32[128,128]{1,0:T(8,128)S(1)}, f32[128,128]{1,0:T(8,128)S(1)}, f32[128,128]{1,0:T(8,128)S(1)}, bf16[3,128,128]{2,1,0:T(8,128)(2,1)S(1)}, f32[...) custom-call(f32[128,128]{1,0:T(8,128)} %refs_0_.1, f32[128,128]{1,0:T(8,128)} %refs_1_.3, ...), custom_call_target="tpu_custom_call" | custom-call | tf_op jit(solution)/shard_map/pallas_call | solution.py:497
  22.7 4.9 %all-to-all-done.received_ref = f32[32,2,128]{2,1,0:T(2,128)S(1)} async-done(((f32[32,2,128]{2,1,0:T(2,128)}), f32[32,2,128]{2,1,0:T(2,128)S(1)}, u32[]{:S(2)}, u32[]{:S(2)}) %all-to-all-start) | async-done | bytes 32800 | tf_op jit(solution)/shard_map/all_to_all | solution.py:483
  27.6 1.0 %shard_map.160 = (f32[128,128]{1,0:T(8,128)}, f32[128,128]{1,0:T(8,128)}, f32[128,128]{1,0:T(8,128)}) custom-call(f32[32,2,128]{2,1,0:T(2,128)S(1)} %all-to-all-done.received_ref, f32[2,4,128]{2,1,0:T(4,128)S(1)} %all-gather.1.inner_ref, f32[1,128]{1,0:T(1,128)S(1)} %get-tuple-element.24.outer_ref, f32[8,128]{1,0:T(8,128)S(1)} %get-tuple-element.21.refs_10_.vectors_ref, ...), custom_call_target="tpu_custom_call" | custom-call | tf_op jit(solution)/shard_map/pallas_call | solution.py:507
Async XLA Ops:
  5.5 22.1 %all-to-all-start = ((f32[32,2,128]{2,1,0:T(2,128)}), f32[32,2,128]{2,1,0:T(2,128)S(1)}, u32[]{:S(2)}, u32[]{:S(2)}) async-start(f32[32,2,128]{2,1,0:T(2,128)} %shard_map.158), calls=%async_computation | async-start | bytes 65536 | tf_op jit(solution)/shard_map/all_to_all | solution.py:483

commit v7 on v5

--- a/solution.py
+++ b/solution.py
@@ -115,9 +115,21 @@
 
 
 def sums_kernel(*refs):
-    count = 11
+    count = 14
     sources, refs = refs[:count], refs[count:]
-    (own_ref, to_inner_ref, to_outer_ref, interim_ref, vectors_ref, alpha_ref, beta_ref), refs = refs[:7], refs[7:]
+    (
+        own_ref,
+        to_inner_ref,
+        to_outer_ref,
+        vectors_ref,
+        wet_ref,
+        zonal_part_ref,
+        meridional_part_ref,
+        green_ref,
+        solved_ref,
+        take_ref,
+        outer_ref,
+    ), refs = refs[:11], refs[11:]
     held, rows_ref, arrived = refs[:count], refs[count], refs[count + 1]
     copies = load(sources, held, arrived)
     (
@@ -132,6 +144,9 @@
         meridional_ref,
         height_old_ref,
         metric_ref,
+        coriolis_ref,
+        zonal_old_ref,
+        meridional_old_ref,
     ) = held
     columns, rows = height_now_ref.shape
     blocks = weight_ref.shape[0]
@@ -185,14 +200,25 @@
         jnp.where(place == 0, low_p, jnp.where(place == rows - 1, high_p, 0.0)),
         jnp.where(place == 0, low_q, jnp.where(place == rows - 1, high_q, 0.0)),
     )
-    alpha_ref[...] = 1.0 / p_end
-    beta_ref[...] = 1.0 / q_end
+
+    from_south = running_product(jnp.where(row < block, 1.0 / p_end, 1.0), -1)
+    from_north = running_product(jnp.where(row > block, 1.0 / q_end, 1.0), 1)
+    weights = (
+        jnp.where(row < block, from_south, 0.0),
+        jnp.where(row == block - 1, 1.0, 0.0),
+        jnp.where(row > block, from_north, 0.0),
+        jnp.where(row == block + 1, 1.0, 0.0),
+    )
+    for source in range(blocks):
+        for index, values in enumerate(weights):
+            take_ref[source, index : index + 1, :] = values[source : source + 1, :]
     for index, values in enumerate(stacked):
         rows_ref[index] = values
         vectors_ref[index : index + 1, :] = rows_ref[index, pl.ds(block, 1), :]
 
     shape = (columns, rows)
     subs = iota(shape, 0)
+    lanes = iota(shape, 1)
     added = jnp.zeros(shape, F32)
     parts = thirds(amount_ref[...])
     chunks = range(lon_ref.shape[0])
@@ -204,7 +230,8 @@
         amounts = jnp.concatenate([jnp.where(here[i], part[i : i + 1, :], 0.0) for i in chunks], axis=1)
         added += dot(amounts.astype(BF16), there, (1, 1), None)
 
-    depth = depth_ref[...] * land_ref[...].astype(F32)
+    wet = land_ref[...].astype(F32)
+    depth = depth_ref[...] * wet
     flux_east = depth * zonal_ref[...]
     flux_north = depth * meridional_ref[...]
     metric = metric_ref[...]
@@ -213,7 +240,6 @@
         - COURANT * (metric * differences(flux_east, 0) + differences(flux_north, 1))
         + added
     )
-    interim_ref[...] = interim
 
     eight = iota((8, rows), 0)
     along = iota((8, rows), 1)
@@ -221,7 +247,6 @@
     on_interim = jnp.where(eight < 2, vectors, 0.0)
     on_edges = jnp.where(eight < 2, pltpu.roll(vectors, 2, 0), 0.0)
     on_edges += jnp.where((eight == 2) & (along == 1) | (eight == 3) & (along == 2), 1.0, 0.0)
-    lanes = iota(shape, 1)
     edges = jnp.where((lanes == 0) | (lanes == rows - 1), flux_north, pltpu.roll(height_now_ref[...], 2, 1))
     total = sums_dot(
         jnp.concatenate([on_interim, on_edges], axis=1), jnp.concatenate([interim, edges], axis=1)
@@ -239,6 +264,33 @@
     to_east = jnp.where(eight < 2, to_east, jnp.where(eight == 2, height_now_ref[last:columns, :], flux_last))
     to_inner_ref[...] = jnp.where(odd, to_west, to_east)[0:4]
     to_outer_ref[...] = jnp.where(odd, to_east, to_west)[0:4]
+
+    p_from = jnp.broadcast_to(vectors[0:1, :], shape).T
+    q_from = jnp.broadcast_to(vectors[1:2, :], shape).T
+    green = thirds(jnp.where(subs <= lanes, p_from * vectors[2:3, :], q_from * vectors[3:4, :]))
+    for index, part in enumerate(green):
+        green_ref[index] = part.astype(BF16)
+    parts = thirds(interim)
+    pairs = [(i, j) for i in range(3) for j in range(3 - i)]
+    solved = dot(
+        jnp.concatenate([parts[i] for i, _ in pairs], axis=1).astype(BF16),
+        jnp.concatenate([green[j] for _, j in pairs], axis=0).astype(BF16),
+        (1, 0),
+        None,
+    )
+    solved += flux_north[:, 0:1] * vectors[4:5, :] + flux_north[:, rows - 1 : rows] * vectors[5:6, :]
+    solved_ref[...] = wet * solved
+
+    height = height_now_ref[...]
+    outer_ref[...] = COURANT * metric
+    turning = coriolis_ref[...]
+    wet_ref[...] = wet
+    zonal_part_ref[...] = wet * (
+        zonal_old_ref[...] - COURANT * metric * differences(height, 0) + turning * meridional_ref[...]
+    )
+    meridional_part_ref[...] = wet * (
+        meridional_old_ref[...] - COURANT * differences(height, 1) - turning * zonal_ref[...]
+    )
 
 
 def pack_kernel(own_ref, inner_ref, to_outer_ref, send_ref):
@@ -260,71 +312,6 @@
         send_ref[at_own + slot] = jnp.where(north, own_up, own_down)
         send_ref[at_outer + slot] = jnp.where(north, outer_up, outer_down)
     send_ref[at_outer + blocks - 1 - block] = outer[2:4]
-
-
-def local_kernel(*refs):
-    count = 9
-    sources, refs = refs[:count], refs[count:]
-    (interim_ref, vectors_ref, alpha_ref, beta_ref), refs = refs[:4], refs[4:]
-    (wet_ref, zonal_part_ref, meridional_part_ref, green_ref, solved_ref, take_ref, outer_ref), refs = refs[:7], refs[7:]
-    held, arrived = refs[:count], refs[count]
-    copies = load(sources, held, arrived)
-    (
-        height_now_ref,
-        zonal_ref,
-        depth_ref,
-        land_ref,
-        meridional_ref,
-        metric_ref,
-        coriolis_ref,
-        zonal_old_ref,
-        meridional_old_ref,
-    ) = held
-    shape = height_now_ref.shape
-    rows = shape[1]
-    subs = iota(shape, 0)
-    lanes = iota(shape, 1)
-    blocks = alpha_ref.shape[0]
-    block = lax.axis_index("lat")
-
-    row = iota(alpha_ref.shape, 0)
-    from_south = running_product(jnp.where(row < block, alpha_ref[...], 1.0), -1)
-    from_north = running_product(jnp.where(row > block, beta_ref[...], 1.0), 1)
-    weights = (
-        jnp.where(row < block, from_south, 0.0),
-        jnp.where(row == block - 1, 1.0, 0.0),
-        jnp.where(row > block, from_north, 0.0),
-        jnp.where(row == block + 1, 1.0, 0.0),
-    )
-    for source in range(blocks):
-        for index, values in enumerate(weights):
-            take_ref[source, index : index + 1, :] = values[source : source + 1, :]
-
-    for copy in copies:
-        copy.wait()
-    wet = land_ref[...].astype(F32)
-    flux_north = depth_ref[...] * wet * meridional_ref[...]
-
-    vectors = vectors_ref[...]
-    p_from = jnp.broadcast_to(vectors[0:1, :], shape).T
-    q_from = jnp.broadcast_to(vectors[1:2, :], shape).T
-    green = jnp.where(subs <= lanes, p_from * vectors[2:3, :], q_from * vectors[3:4, :])
-    for index, part in enumerate(thirds(green)):
-        green_ref[index] = part.astype(BF16)
-    solved = dot(interim_ref[...], green, (1, 0))
-    solved += flux_north[:, 0:1] * vectors[4:5, :] + flux_north[:, rows - 1 : rows] * vectors[5:6, :]
-    solved_ref[...] = wet * solved
-
-    height = height_now_ref[...]
-    outer_ref[...] = COURANT * metric_ref[...]
-    turning = coriolis_ref[...]
-    wet_ref[...] = wet
-    zonal_part_ref[...] = wet * (
-        zonal_old_ref[...] - COURANT * metric_ref[...] * differences(height, 0) + turning * meridional_ref[...]
-    )
-    meridional_part_ref[...] = wet * (
-        meridional_old_ref[...] - COURANT * differences(height, 1) - turning * zonal_ref[...]
-    )
 
 
 def finish_kernel(
@@ -379,10 +366,7 @@
         south += take[0:2] * values
         north += take[2:4] * values
     onto = jnp.concatenate([south, north, jnp.zeros((4, columns), F32)], axis=0)
-    onto = jnp.where((eight == 4) & (along == 0) | (eight == 5) & (along == last), 1.0, onto)
-    heights = select_rows(
-        eight, (vectors_ref[2:3, :], 0.0, vectors_ref[3:4, :], 0.0, outer_rows, outer_rows)
-    )
+    heights = select_rows(eight, (vectors_ref[2:3, :], 0.0, vectors_ref[3:4, :]))
     sides = jnp.where(
         (eight == 1) & (along == 0), COURANT, jnp.where((eight == 3) & (along == rows - 1), -COURANT, 0.0)
     )
@@ -396,6 +380,8 @@
         None,
     )
     height_ref[...] = solved_ref[...] + wet * both[:, :rows]
+    height_ref[0:1, :] += wet_ref[0:1, :] * outer_rows[4:5]
+    height_ref[last:columns, :] += wet_ref[last:columns, :] * outer_rows[5:6]
     meridional_ref[...] = meridional_part_ref[...] + wet * both[:, rows:]
 
 
@@ -441,27 +427,28 @@
     def pinned(values):
         return pltpu.with_memory_space_constraint(values, pltpu.HBM)
 
-    height_now, zonal_now, ocean_depth, land_sea, meridional_now, metric = (
-        pinned(x) for x in (height_now, zonal_now, ocean_depth, land_sea, meridional_now, metric_factor[None, :])
-    )
     read = (
         pinned(implicit_weight.reshape(blocks, rows)),
-        height_now,
-        zonal_now,
-        ocean_depth,
-        land_sea,
+        pinned(height_now),
+        pinned(zonal_now),
+        pinned(ocean_depth),
+        pinned(land_sea),
         pinned(source_longitude.reshape(-1, rows)),
         pinned(source_latitude.reshape(-1, rows)),
         pinned(source_amplitude.reshape(-1, rows)),
-        meridional_now,
+        pinned(meridional_now),
         pinned(height_old),
-        metric,
+        pinned(metric_factor[None, :]),
+        pinned(coriolis[None, :]),
+        pinned(zonal_old),
+        pinned(meridional_old),
     )
     held, arrived = loading(read)
-    own, to_inner, to_outer, interim, vectors, alpha, beta = call(
+    block = kept(columns, rows)
+    own, to_inner, to_outer, vectors, wet, zonal_part, meridional_part, green, solved, take, outer = call(
         sums_kernel,
-        [kept(4, columns), kept(4, columns), kept(4, columns), kept(columns, rows)]
-        + [kept(8, rows), kept(blocks, rows), kept(blocks, rows)],
+        [kept(4, columns), kept(4, columns), kept(4, columns), kept(8, rows), block, block, block]
+        + [pltpu.VMEM((3, rows, rows), BF16), block, kept(blocks, 4, rows), kept(1, rows)],
         [HBM] * len(read),
         [*held, pltpu.VMEM((8, blocks, rows), F32), arrived],
     )(*read)
@@ -476,26 +463,6 @@
     (send,) = call(pack_kernel, [kept(2 * blocks, 2, columns)], [VMEM] * 3)(own, inner, to_outer)
     received = lax.all_to_all(send, ("lon", "lat"), 0, 0, axis_index_groups=groups, tiled=True)
 
-    read = (
-        height_now,
-        zonal_now,
-        ocean_depth,
-        land_sea,
-        meridional_now,
-        metric,
-        pinned(coriolis[None, :]),
-        pinned(zonal_old),
-        pinned(meridional_old),
-    )
-    held, arrived = loading(read)
-    wet, zonal_part, meridional_part, green, solved, take, outer = call(
-        local_kernel,
-        [kept(columns, rows)] * 3
-        + [pltpu.VMEM((3, rows, rows), BF16), kept(columns, rows), kept(blocks, 4, rows), kept(1, rows)],
-        [HBM] * len(read) + [VMEM] * 4,
-        [*held, arrived],
-    )(*read, interim, vectors, alpha, beta)
-
     block = jax.ShapeDtypeStruct((columns, rows), F32)
     return tuple(
         call(finish_kernel, [block] * 3, [VMEM] * 10)(

time: 28.6 us -> 27.6 us (0.965)
  the two profiles are of different devices: /device:TPU:31 before, /device:TPU:4 now
where the time goes in v7:
time: 27.6 us; the launch traced here: 27.4 us
  blocking collectives  23.5 us (85%)
  Pallas kernels  3.25 us (12%)
  between operations  0.65 us (2%)
    all_to_all x1, blocking collectives, per_device(): lax.all_to_all(send, ('lon', 'lat'), 0, 0, axis_index_groups=groups, tile...  21.7 us
    pallas_call x1, Pallas kernels, per_device(): call(sums_kernel, [kept(4, columns), kept(4, columns), kept(4, columns),...  2.34 us
    all_gather x1, blocking collectives, per_device(): inner = lax.all_gather(to_inner, 'lon', axis=0, axis_index_groups=pairs)  1.78 us
    pallas_call x1, Pallas kernels, per_device(): call(finish_kernel, [block] * 3, [VMEM] * 10)  0.89 us

profile of v7, /device:TPU:4, one launch (start us, length us, event | category | flops | bytes accessed | tf_op | source)
XLA Modules:
  0.0 27.4 jit_solution(5254166918040546078)
XLA Ops:
  0.6 2.3 %shard_map.157 = (f32[4,128]{1,0:T(4,128)S(1)}, f32[4,128]{1,0:T(4,128)S(1)}, f32[4,128]{1,0:T(4,128)S(1)}, f32[8,128]{1,0:T(8,128)S(1)}, f32[128,128]{1,0:T(8,1...) custom-call(f32[16,128]{1,0:T(8,128)} %bitcast.8, ...), custom_call_target="tpu_custom_call" | custom-call | tf_op jit(solution)/shard_map/pallas_call | solution.py:448
  3.0 1.8 %all-gather.1.inner_ref = f32[2,4,128]{2,1,0:T(4,128)S(1)} all-gather(f32[1,4,128]{2,1,0:T(4,128)S(1)} %bitcast.7), channel_id=2, replica_groups={{0,16},{32,48},{64,80},{96,112},{128,144},{160,176},{192,208},{224,240}..., dimensions={0}, use_global_device_ids=true | all-gather | bytes 6144 | tf_op jit(solution)/shard_map/all_gather | solution.py:457
  4.8 21.7 %all_to_all.5.received_ref = f32[32,2,128]{2,1,0:T(2,128)S(1)} all-to-all(f32[32,2,128]{2,1,0:T(2,128)S(1)} %shard_map.158), channel_id=1, replica_groups={{47,46,45,44,43,42,41,40,39,38,37,36,35,34,33,32,31,30,29,28,27,26,25,2..., dimensions={0} | all-to-all | bytes 65536 | tf_op jit(solution)/shard_map/all_to_all | solution.py:464
  26.5 0.9 %shard_map.159 = (f32[128,128]{1,0:T(8,128)}, f32[128,128]{1,0:T(8,128)}, f32[128,128]{1,0:T(8,128)}) custom-call(f32[32,2,128]{2,1,0:T(2,128)S(1)} %all_to_all.5.received_ref, f32[2,4,128]{2,1,0:T(4,128)S(1)} %all-gather.1.inner_ref, f32[1,128]{1,0:T(1,128)S(1)} %get-tuple-element.17.outer_ref, f32[8,128]{1,0:T(8,128)S(1)} %get-tuple-element.18.vectors_ref, ...), custom_call_target="tpu_custom_call" | custom-call | tf_op jit(solution)/shard_map/pallas_call | solution.py:468
  (1 shorter events, 0.0 us)

commit v8 on v7

--- a/solution.py
+++ b/solution.py
@@ -297,7 +297,6 @@
     blocks = send_ref.shape[0] // 2
     block = lax.axis_index("lat")
     parity = lax.axis_index("lon") & 1
-    at_own, at_outer = parity * blocks, (1 - parity) * blocks
     own = own_ref[...]
     row = iota(own.shape, 0)
     own += jnp.where(row < 2, inner_ref[1 - parity], 0.0)
@@ -308,10 +307,10 @@
     outer_down = jnp.concatenate([outer[1:2], jnp.zeros_like(outer[0:1])], axis=0)
     for target in range(blocks):
         north = jnp.full(own_up.shape, (block < target).astype(jnp.int32), jnp.int32) == 1
-        slot = blocks - 1 - target
-        send_ref[at_own + slot] = jnp.where(north, own_up, own_down)
-        send_ref[at_outer + slot] = jnp.where(north, outer_up, outer_down)
-    send_ref[at_outer + blocks - 1 - block] = outer[2:4]
+        slot = 2 * (blocks - 1 - target)
+        send_ref[slot + 1 - parity] = jnp.where(north, own_up, own_down)
+        send_ref[slot + parity] = jnp.where(north, outer_up, outer_down)
+    send_ref[2 * (blocks - 1 - block) + parity] = outer[2:4]
 
 
 def finish_kernel(
@@ -338,10 +337,9 @@
     along = iota((8, columns), 1)
     block = lax.axis_index("lat")
     parity = lax.axis_index("lon") & 1
-    at_own, at_other = parity * blocks, (1 - parity) * blocks
 
     inner = inner_ref[1 - parity][2:4]
-    other = received_ref[at_other + blocks - 1 - block]
+    other = received_ref[2 * (blocks - 1 - block) + parity]
     odd = jnp.full(other.shape, parity, jnp.int32) == 1
     west = jnp.where(odd, inner, other)
     east = jnp.where(odd, other, inner)
@@ -360,8 +358,8 @@
     south = jnp.zeros(other.shape, F32)
     north = jnp.zeros(other.shape, F32)
     for source in range(blocks):
-        slot = blocks - 1 - source
-        values = received_ref[at_own + slot] + received_ref[at_other + slot]
+        slot = 2 * (blocks - 1 - source)
+        values = received_ref[slot] + received_ref[slot + 1]
         take = take_ref[source]
         south += take[0:2] * values
         north += take[2:4] * values
@@ -457,7 +455,7 @@
     inner = lax.all_gather(to_inner, "lon", axis=0, axis_index_groups=pairs)
 
     groups = [
-        [lon * blocks + lat for lon in ((first + 1) % around, first) for lat in reversed(range(blocks))]
+        [lon * blocks + lat for lat in reversed(range(blocks)) for lon in (first, (first + 1) % around)]
         for first in range(1, around, 2)
     ]
     (send,) = call(pack_kernel, [kept(2 * blocks, 2, columns)], [VMEM] * 3)(own, inner, to_outer)

time: 27.6 us -> 28.2 us (1.022)
  the two profiles are of different devices: /device:TPU:4 before, /device:TPU:27 now
where the time goes in v8:
time: 28.2 us; the launch traced here: 28 us
  blocking collectives  24.1 us (85%)
  Pallas kernels  3.25 us (12%)
  between operations  0.65 us (2%)
    all_to_all x1, blocking collectives, per_device(): lax.all_to_all(send, ('lon', 'lat'), 0, 0, axis_index_groups=groups, tile...  21.9 us
    pallas_call x1, Pallas kernels, per_device(): call(sums_kernel, [kept(4, columns), kept(4, columns), kept(4, columns),...  2.34 us
    all_gather x1, blocking collectives, per_device(): inner = lax.all_gather(to_inner, 'lon', axis=0, axis_index_groups=pairs)  2.15 us
    pallas_call x1, Pallas kernels, per_device(): call(finish_kernel, [block] * 3, [VMEM] * 10)  0.88 us

profile of v8, /device:TPU:27, one launch (start us, length us, event | category | flops | bytes accessed | tf_op | source)
XLA Modules:
  0.0 28.0 jit_solution(12996020573489645808)
XLA Ops:
  0.6 2.3 %shard_map.157 = (f32[4,128]{1,0:T(4,128)S(1)}, f32[4,128]{1,0:T(4,128)S(1)}, f32[4,128]{1,0:T(4,128)S(1)}, f32[8,128]{1,0:T(8,128)S(1)}, f32[128,128]{1,0:T(8,1...) custom-call(f32[16,128]{1,0:T(8,128)} %bitcast.8, ...), custom_call_target="tpu_custom_call" | custom-call | tf_op jit(solution)/shard_map/pallas_call | solution.py:446
  3.0 2.2 %all-gather.1.inner_ref = f32[2,4,128]{2,1,0:T(4,128)S(1)} all-gather(f32[1,4,128]{2,1,0:T(4,128)S(1)} %bitcast.7), channel_id=2, replica_groups={{0,16},{32,48},{64,80},{96,112},{128,144},{160,176},{192,208},{224,240}..., dimensions={0}, use_global_device_ids=true | all-gather | bytes 6144 | tf_op jit(solution)/shard_map/all_gather | solution.py:455
  5.2 21.9 %all_to_all.5.received_ref = f32[32,2,128]{2,1,0:T(2,128)S(1)} all-to-all(f32[32,2,128]{2,1,0:T(2,128)S(1)} %shard_map.158), channel_id=1, replica_groups={{31,47,30,46,29,45,28,44,27,43,26,42,25,41,24,40,23,39,22,38,21,37,20,3..., dimensions={0} | all-to-all | bytes 65536 | tf_op jit(solution)/shard_map/all_to_all | solution.py:462
  27.1 0.9 %shard_map.159 = (f32[128,128]{1,0:T(8,128)}, f32[128,128]{1,0:T(8,128)}, f32[128,128]{1,0:T(8,128)}) custom-call(f32[32,2,128]{2,1,0:T(2,128)S(1)} %all_to_all.5.received_ref, f32[2,4,128]{2,1,0:T(4,128)S(1)} %all-gather.1.inner_ref, f32[1,128]{1,0:T(1,128)S(1)} %get-tuple-element.17.outer_ref, f32[8,128]{1,0:T(8,128)S(1)} %get-tuple-element.18.vectors_ref, ...), custom_call_target="tpu_custom_call" | custom-call | tf_op jit(solution)/shard_map/pallas_call | solution.py:466
  (1 shorter events, 0.0 us)

commit v9 on v8

--- a/solution.py
+++ b/solution.py
@@ -80,6 +80,14 @@
     after = jnp.where(place == size - 1, 0.0, pltpu.roll(values, size - 1, axis))
     before = jnp.where(place == 0, 0.0, pltpu.roll(values, 1, axis))
     return after - before
+
+
+def place(lat, blocks):
+    half = blocks // 2
+    if isinstance(lat, int):
+        return (2 * (blocks - 1 - lat), 1) if lat >= half else (blocks + half - 1 - lat, half)
+    north = lat >= half
+    return jnp.where(north, 2 * (blocks - 1 - lat), blocks + half - 1 - lat), jnp.where(north, 1, half)
 
 
 def load(sources, held, arrived):
@@ -307,10 +315,11 @@
     outer_down = jnp.concatenate([outer[1:2], jnp.zeros_like(outer[0:1])], axis=0)
     for target in range(blocks):
         north = jnp.full(own_up.shape, (block < target).astype(jnp.int32), jnp.int32) == 1
-        slot = 2 * (blocks - 1 - target)
-        send_ref[slot + 1 - parity] = jnp.where(north, own_up, own_down)
-        send_ref[slot + parity] = jnp.where(north, outer_up, outer_down)
-    send_ref[2 * (blocks - 1 - block) + parity] = outer[2:4]
+        slot, step = place(target, blocks)
+        send_ref[slot + step * parity] = jnp.where(north, own_up, own_down)
+        send_ref[slot + step * (1 - parity)] = jnp.where(north, outer_up, outer_down)
+    slot, step = place(block, blocks)
+    send_ref[slot + step * (1 - parity)] = outer[2:4]
 
 
 def finish_kernel(
@@ -337,9 +346,10 @@
     along = iota((8, columns), 1)
     block = lax.axis_index("lat")
     parity = lax.axis_index("lon") & 1
+    slot, step = place(block, blocks)
 
     inner = inner_ref[1 - parity][2:4]
-    other = received_ref[2 * (blocks - 1 - block) + parity]
+    other = received_ref[slot + step * (1 - parity)]
     odd = jnp.full(other.shape, parity, jnp.int32) == 1
     west = jnp.where(odd, inner, other)
     east = jnp.where(odd, other, inner)
@@ -358,8 +368,8 @@
     south = jnp.zeros(other.shape, F32)
     north = jnp.zeros(other.shape, F32)
     for source in range(blocks):
-        slot = 2 * (blocks - 1 - source)
-        values = received_ref[slot] + received_ref[slot + 1]
+        slot, step = place(source, blocks)
+        values = received_ref[slot] + received_ref[slot + step]
         take = take_ref[source]
         south += take[0:2] * values
         north += take[2:4] * values
@@ -454,8 +464,10 @@
     pairs = [[i, i + 1] for i in range(0, around, 2)]
     inner = lax.all_gather(to_inner, "lon", axis=0, axis_index_groups=pairs)
 
+    members = [(odd, lat) for lat in range(blocks) for odd in (0, 1)]
+    members.sort(key=lambda m: place(m[1], blocks)[0] + place(m[1], blocks)[1] * m[0])
     groups = [
-        [lon * blocks + lat for lat in reversed(range(blocks)) for lon in (first, (first + 1) % around)]
+        [(first + 1 - odd) % around * blocks + lat for odd, lat in members]
         for first in range(1, around, 2)
     ]
     (send,) = call(pack_kernel, [kept(2 * blocks, 2, columns)], [VMEM] * 3)(own, inner, to_outer)

time: 28.2 us -> 27.5 us (0.975)
  the two profiles are of different devices: /device:TPU:27 before, /device:TPU:4 now
where the time goes in v9:
time: 27.5 us; the launch traced here: 27.3 us
  blocking collectives  23.4 us (85%)
  Pallas kernels  3.24 us (12%)
  between operations  0.65 us (2%)
    all_to_all x1, blocking collectives, per_device(): lax.all_to_all(send, ('lon', 'lat'), 0, 0, axis_index_groups=groups, tile...  21.6 us
    pallas_call x1, Pallas kernels, per_device(): call(sums_kernel, [kept(4, columns), kept(4, columns), kept(4, columns),...  2.34 us
    all_gather x1, blocking collectives, per_device(): inner = lax.all_gather(to_inner, 'lon', axis=0, axis_index_groups=pairs)  1.78 us
    pallas_call x1, Pallas kernels, per_device(): call(finish_kernel, [block] * 3, [VMEM] * 10)  0.88 us

profile of v9, /device:TPU:4, one launch (start us, length us, event | category | flops | bytes accessed | tf_op | source)
XLA Modules:
  0.0 27.3 jit_solution(4282219348623975977)
XLA Ops:
  0.6 2.3 %shard_map.157 = (f32[4,128]{1,0:T(4,128)S(1)}, f32[4,128]{1,0:T(4,128)S(1)}, f32[4,128]{1,0:T(4,128)S(1)}, f32[8,128]{1,0:T(8,128)S(1)}, f32[128,128]{1,0:T(8,1...) custom-call(f32[16,128]{1,0:T(8,128)} %bitcast.8, ...), custom_call_target="tpu_custom_call" | custom-call | tf_op jit(solution)/shard_map/pallas_call | solution.py:456
  3.0 1.8 %all-gather.1.inner_ref = f32[2,4,128]{2,1,0:T(4,128)S(1)} all-gather(f32[1,4,128]{2,1,0:T(4,128)S(1)} %bitcast.7), channel_id=2, replica_groups={{0,16},{32,48},{64,80},{96,112},{128,144},{160,176},{192,208},{224,240}..., dimensions={0}, use_global_device_ids=true | all-gather | bytes 6144 | tf_op jit(solution)/shard_map/all_gather | solution.py:465
  4.8 21.6 %all_to_all.5.received_ref = f32[32,2,128]{2,1,0:T(2,128)S(1)} all-to-all(f32[32,2,128]{2,1,0:T(2,128)S(1)} %shard_map.158), channel_id=1, replica_groups={{47,31,46,30,45,29,44,28,43,27,42,26,41,25,40,24,39,38,37,36,35,34,33,3..., dimensions={0} | all-to-all | bytes 65536 | tf_op jit(solution)/shard_map/all_to_all | solution.py:474
  26.4 0.9 %shard_map.159 = (f32[128,128]{1,0:T(8,128)}, f32[128,128]{1,0:T(8,128)}, f32[128,128]{1,0:T(8,128)}) custom-call(f32[32,2,128]{2,1,0:T(2,128)S(1)} %all_to_all.5.received_ref, f32[2,4,128]{2,1,0:T(4,128)S(1)} %all-gather.1.inner_ref, f32[1,128]{1,0:T(1,128)S(1)} %get-tuple-element.17.outer_ref, f32[8,128]{1,0:T(8,128)S(1)} %get-tuple-element.18.vectors_ref, ...), custom_call_target="tpu_custom_call" | custom-call | tf_op jit(solution)/shard_map/pallas_call | solution.py:478
  (1 shorter events, 0.0 us)

commit v10 on v9

--- a/solution.py
+++ b/solution.py
@@ -162,8 +162,7 @@
     first_east = lax.axis_index("lon") * columns
     first_north = block * rows
 
-    for copy in copies:
-        copy.wait()
+    copies[0].wait()
     c = 1.0 / weight_ref[...]
     one = jnp.ones_like(c)
     mats = (1.0 + c, one, c, one)
@@ -224,6 +223,8 @@
         rows_ref[index] = values
         vectors_ref[index : index + 1, :] = rows_ref[index, pl.ds(block, 1), :]
 
+    for copy in copies[1:]:
+        copy.wait()
     shape = (columns, rows)
     subs = iota(shape, 0)
     lanes = iota(shape, 1)

time: 27.5 us -> 27.2 us (0.989)
  Pallas kernels: 3.24 us -> 2.94 us
    pallas_call x1, Pallas kernels: 2.34 us -> 2.04 us  [per_device(): call(sums_kernel, [kept(4, columns), kept(4, columns), kept(4, columns),...]
where the time goes in v10:
time: 27.2 us; the launch traced here: 27 us
  blocking collectives  23.4 us (86%)
  Pallas kernels  2.94 us (11%)
  between operations  0.65 us (2%)
    all_to_all x1, blocking collectives, per_device(): lax.all_to_all(send, ('lon', 'lat'), 0, 0, axis_index_groups=groups, tile...  21.6 us
    pallas_call x1, Pallas kernels, per_device(): call(sums_kernel, [kept(4, columns), kept(4, columns), kept(4, columns),...  2.04 us
    all_gather x1, blocking collectives, per_device(): inner = lax.all_gather(to_inner, 'lon', axis=0, axis_index_groups=pairs)  1.78 us
    pallas_call x1, Pallas kernels, per_device(): call(finish_kernel, [block] * 3, [VMEM] * 10)  0.88 us

profile of v10, /device:TPU:4, one launch (start us, length us, event | category | flops | bytes accessed | tf_op | source)
XLA Modules:
  0.0 27.0 jit_solution(7965061091390313314)
XLA Ops:
  0.6 2.0 %shard_map.157 = (f32[4,128]{1,0:T(4,128)S(1)}, f32[4,128]{1,0:T(4,128)S(1)}, f32[4,128]{1,0:T(4,128)S(1)}, f32[8,128]{1,0:T(8,128)S(1)}, f32[128,128]{1,0:T(8,1...) custom-call(f32[16,128]{1,0:T(8,128)} %bitcast.8, ...), custom_call_target="tpu_custom_call" | custom-call | tf_op jit(solution)/shard_map/pallas_call | solution.py:457
  2.7 1.8 %all-gather.1.inner_ref = f32[2,4,128]{2,1,0:T(4,128)S(1)} all-gather(f32[1,4,128]{2,1,0:T(4,128)S(1)} %bitcast.7), channel_id=2, replica_groups={{0,16},{32,48},{64,80},{96,112},{128,144},{160,176},{192,208},{224,240}..., dimensions={0}, use_global_device_ids=true | all-gather | bytes 6144 | tf_op jit(solution)/shard_map/all_gather | solution.py:466
  4.5 21.6 %all_to_all.5.received_ref = f32[32,2,128]{2,1,0:T(2,128)S(1)} all-to-all(f32[32,2,128]{2,1,0:T(2,128)S(1)} %shard_map.158), channel_id=1, replica_groups={{47,31,46,30,45,29,44,28,43,27,42,26,41,25,40,24,39,38,37,36,35,34,33,3..., dimensions={0} | all-to-all | bytes 65536 | tf_op jit(solution)/shard_map/all_to_all | solution.py:475
  26.1 0.9 %shard_map.159 = (f32[128,128]{1,0:T(8,128)}, f32[128,128]{1,0:T(8,128)}, f32[128,128]{1,0:T(8,128)}) custom-call(f32[32,2,128]{2,1,0:T(2,128)S(1)} %all_to_all.5.received_ref, f32[2,4,128]{2,1,0:T(4,128)S(1)} %all-gather.1.inner_ref, f32[1,128]{1,0:T(1,128)S(1)} %get-tuple-element.17.outer_ref, f32[8,128]{1,0:T(8,128)S(1)} %get-tuple-element.18.vectors_ref, ...), custom_call_target="tpu_custom_call" | custom-call | tf_op jit(solution)/shard_map/pallas_call | solution.py:479
  (1 shorter events, 0.0 us)
